TPU v7x, 32 devices: a whole 2x2x4 slice. The times are simulated.
32 devices in a mesh: dp: 4 (over y, core), gx: 4 (over z), gy: 2 (over x).
Axes of the slice: x: 2, y: 2, z: 4, core: 2. Of those that a mesh axis runs over, the one named last changes fastest.
Arguments:
- stream_in: bfloat16 [12288, 2048], P(('dp', 'gx'), 'gy'), may hold values from -11 to 11
- lengths: int32 [8], P('dp'), may hold values from 1024 to 1536, as said below
- routes: int32 [12288, 4], P('dp'), may hold values from 0 to 15, all different within a row; in each aligned block of 3072 rows (0 to 3071, 3072 to 6143, ...) at most 1152 rows name the same one
- route_weights: float32 [12288, 4], P('dp'), may hold values from 0.15 to 0.6
- norm_attn: bfloat16 [2048], P('gy'), may hold values from 0.5 to 1.5
- w_qkv: bfloat16 [2048, 16, 384], P('gy', 'gx'), may hold values from -0.125 to 0.125
- qkv_bias: bfloat16 [16, 384], P('gx'), may hold values from -1 to 1
- w_out: bfloat16 [2048, 2048], P('gx', 'gy'), may hold values from -1 to 1
- norm_ffn: bfloat16 [2048], P('gy'), may hold values from 0.5 to 1.5
- w_gate: bfloat16 [16, 2048, 1408], P(None, 'gy', 'gx'), may hold values from -0.125 to 0.125
- w_up: bfloat16 [16, 2048, 1408], P(None, 'gy', 'gx'), may hold values from -0.125 to 0.125
- w_down: bfloat16 [16, 1408, 2048], P(None, 'gx', 'gy'), may hold values from -0.15625 to 0.15625
- shared_gate: bfloat16 [2048, 5632], P('gy', 'gx'), may hold values from -0.125 to 0.125
- shared_up: bfloat16 [2048, 5632], P('gy', 'gx'), may hold values from -0.125 to 0.125
- shared_down: bfloat16 [5632, 2048], P('gx', 'gy'), may hold values from -0.078125 to 0.078125
- shared_router: bfloat16 [2048], P('gy'), may hold values from -0.125 to 0.125
- cotangent: bfloat16 [12288, 2048], P(('dp', 'gx'), 'gy'), may hold values from -6 to 6
Outputs:
- layer_out: bfloat16 [12288, 2048], P(('dp', 'gx'), 'gy')
- grad_stream: float32 [12288, 2048], P(('dp', 'gx'), 'gy')
- grad_norm_attn: float32 [2048], P('gy')
- grad_w_qkv: float32 [2048, 16, 384], P('gy', 'gx')
- grad_qkv_bias: float32 [16, 384], P('gx')
- grad_w_out: float32 [2048, 2048], P('gx', 'gy')
- grad_norm_ffn: float32 [2048], P('gy')
- grad_w_gate: float32 [16, 2048, 1408], P(None, 'gy', 'gx')
- grad_w_up: float32 [16, 2048, 1408], P(None, 'gy', 'gx')
- grad_w_down: float32 [16, 1408, 2048], P(None, 'gx', 'gy')
- grad_shared_gate: float32 [2048, 5632], P('gy', 'gx')
- grad_shared_up: float32 [2048, 5632], P('gy', 'gx')
- grad_shared_down: float32 [5632, 2048], P('gx', 'gy')
- grad_shared_router: float32 [2048], P('gy')
- rms_stats: float32 [4], replicated
Inputs may be any that keep to these rules, and one draw needn't show every extreme that they name: `lengths`: entries of one group are in slot order; in every group one sequence has exactly 1536 tokens and another exactly 1024, the others lie between; the group's slots after its last sequence are padding. `routes`: each row names 4 different experts; within the 3072 rows of one group no expert is named more than 1152 times.
All inputs are finite; a program needn't handle non-finite values.
Results may differ from a plain program's by a relative error of at most 0.017.
The roundings to bfloat16 on the way count: a program that leaves them out, or rounds other values in their place, can miss the bound.
Values may be sent and summed in bfloat16 or wider, within the bound.
A program may use at most 704 MiB of HBM per device.

v0:
```python
import jax
import jax.numpy as jnp
from jax import lax
from jax.sharding import PartitionSpec as P

D = 2048
HD = 128
TOPK = 4
E = 16
SLOTS = 3072
CAPACITY = 1152


EPS = 1e-06
THETA = 1000000.0
NEG = -1e30


def layout(length_group, slot_count):
    places = jnp.arange(slot_count, dtype=jnp.int32)
    seq_ends = jnp.cumsum(length_group)
    segment = jnp.sum((places[:, None] >= seq_ends[None, :]).astype(jnp.int32), axis=1)
    starts = jnp.concatenate([jnp.zeros((1,), jnp.int32), seq_ends])
    seg_count = starts.shape[0]
    seq_begin = jnp.sum(
        jnp.where(
            segment[:, None] == jnp.arange(seg_count, dtype=jnp.int32)[None, :], starts[None, :], 0
        ),
        axis=1,
    )
    return (segment, places - seq_begin, segment < length_group.shape[0])


def rotary_tables(positions, head_dim):
    half_dim = head_dim // 2
    frequency = THETA ** (-jnp.arange(half_dim, dtype=jnp.float32) * 2.0 / head_dim)
    angles = positions.astype(jnp.float32)[:, None] * frequency[None, :]
    return (jnp.cos(angles), jnp.sin(angles))


def rotate(values, cos_table, sin_table):
    half_dim = values.shape[-1] // 2
    front_half, back_half = (values[..., :half_dim], values[..., half_dim:])
    cosine, sine_part = (cos_table[:, None, :], sin_table[:, None, :])
    return jnp.concatenate(
        [front_half * cosine - back_half * sine_part, back_half * cosine + front_half * sine_part],
        axis=-1,
    )


def rotate_back(gradient, cos_table, sin_table):
    half_dim = gradient.shape[-1] // 2
    front_half, back_half = (gradient[..., :half_dim], gradient[..., half_dim:])
    cosine, sine_part = (cos_table[:, None, :], sin_table[:, None, :])
    return jnp.concatenate(
        [front_half * cosine + back_half * sine_part, back_half * cosine - front_half * sine_part],
        axis=-1,
    )


def dispatch(route_group, weight_group, experts, capacity):
    flat_routes = route_group.reshape(-1)
    onehot = (flat_routes[:, None] == jnp.arange(experts, dtype=jnp.int32)[None, :]).astype(
        jnp.int32
    )
    rank_in = jnp.sum(onehot * (jnp.cumsum(onehot, axis=0) - 1), axis=1)
    slot_of = flat_routes * capacity + rank_in
    owners = jnp.arange(flat_routes.shape[0], dtype=jnp.int32) // route_group.shape[1]
    slot_token = jnp.zeros((experts * capacity,), jnp.int32).at[slot_of].set(owners)
    slot_weight = (
        jnp.zeros((experts * capacity,), jnp.float32).at[slot_of].set(weight_group.reshape(-1))
    )
    slot_used = jnp.zeros((experts * capacity,), jnp.float32).at[slot_of].set(1.0)
    return (slot_of, slot_token, slot_weight, slot_used)


def silu_parts(values):
    logistic = jax.nn.sigmoid(values)
    return (values * logistic, logistic * (1.0 + values * (1.0 - logistic)))


def gather_rows(values):
    return lax.all_gather(values, "gx", axis=0, tiled=True)


def sum_rows(values):
    return lax.psum_scatter(values, "gx", scatter_dimension=0, tiled=True)


def sum_width(values):
    return lax.psum(values, "gy")


def sum_query(values):
    return lax.psum_scatter(values, "gy", scatter_dimension=0, tiled=True)


def gather_query(values):
    return lax.all_gather(values, "gy", axis=0, tiled=True)


def over_blocks(update, running, pieces):
    row_count = pieces[0].shape[0]
    block_rows = 1024
    shaped = tuple(
        (
            member.reshape((row_count // block_rows, block_rows) + member.shape[1:])
            for member in pieces
        )
    )

    def scan_step(carried, scan_item):
        block_index, block_part = scan_item
        return (update(carried, block_part, block_index * block_rows), None)

    running, _ = lax.scan(
        scan_step, running, (jnp.arange(row_count // block_rows, dtype=jnp.int32), shaped)
    )
    return running


def local(
    stream_in,
    lengths,
    routes,
    route_weights,
    norm_attn,
    w_qkv,
    qkv_bias,
    w_out,
    norm_ffn,
    w_gate,
    w_up,
    w_down,
    shared_gate,
    shared_up,
    shared_down,
    shared_router,
    cotangent,
):
    local_rows, width_part = stream_in.shape
    query_rows = SLOTS // lax.axis_size("gy")
    heads_part = w_qkv.shape[1]
    x_index = lax.axis_index("gx")
    y_index = lax.axis_index("gy")
    score_scale = HD ** (-0.5)
    segment, positions, valid_rows = layout(lengths, SLOTS)
    local_valid = lax.dynamic_slice_in_dim(valid_rows, x_index * local_rows, local_rows).astype(
        jnp.float32
    )
    query_start = y_index * query_rows
    places_q = query_start + jnp.arange(query_rows, dtype=jnp.int32)
    segment_q = lax.dynamic_slice_in_dim(segment, query_start, query_rows)
    cos_table, sin_table = rotary_tables(
        lax.dynamic_slice_in_dim(positions, query_start, query_rows), HD
    )
    stream_float = stream_in.astype(jnp.float32)
    inv_attn = lax.rsqrt(sum_width(jnp.sum(stream_float * stream_float, axis=1)) / D + EPS)
    unit_attn = stream_float * inv_attn[:, None]
    gain_attn = norm_attn.astype(jnp.float32)
    normed_all = gather_rows((unit_attn * gain_attn).astype(jnp.bfloat16))
    mixed_rows = sum_query(
        jnp.einsum("td,dhc->thc", normed_all, w_qkv, preferred_element_type=jnp.float32)
    ) + qkv_bias.astype(jnp.float32)
    queries = rotate(mixed_rows[..., :HD], cos_table, sin_table).astype(jnp.bfloat16)
    key_rows = rotate(mixed_rows[..., HD : 2 * HD], cos_table, sin_table).astype(jnp.bfloat16)
    value_rows = mixed_rows[..., 2 * HD :].astype(jnp.bfloat16)

    def scores_for(key_part, offset):
        row_count = key_part.shape[0]
        key_places = offset + jnp.arange(row_count, dtype=jnp.int32)
        key_segment = lax.dynamic_slice_in_dim(segment, offset, row_count)
        allowed = (segment_q[:, None] == key_segment[None, :]) & (
            key_places[None, :] <= places_q[:, None]
        )
        raw_scores = (
            jnp.einsum("qhd,khd->hqk", queries, key_part, preferred_element_type=jnp.float32)
            * score_scale
        )
        return (jnp.where(allowed, raw_scores, NEG), allowed)

    def sweep_keys(update, initial):
        return over_blocks(
            update,
            initial,
            (
                lax.all_gather(key_rows, "gy", axis=0, tiled=True),
                lax.all_gather(value_rows, "gy", axis=0, tiled=True),
            ),
        )

    def stats_step(running, pieces, offset):
        row_max, row_sum = running
        scores, allowed = scores_for(pieces[0], offset)
        new_max = jnp.maximum(row_max, jnp.max(scores, axis=2))
        exp_terms = jnp.where(allowed, jnp.exp(scores - new_max[:, :, None]), 0.0)
        return (new_max, row_sum * jnp.exp(row_max - new_max) + jnp.sum(exp_terms, axis=2))

    start_max = jnp.full((heads_part, query_rows), NEG, jnp.float32)
    row_max, row_sum = sweep_keys(
        stats_step, (start_max, jnp.zeros((heads_part, query_rows), jnp.float32))
    )
    log_total = row_max + jnp.log(row_sum)

    def value_step(running, pieces, offset):
        main_sum, extra_sum = running
        scores, allowed = scores_for(pieces[0], offset)
        prob_rows = jnp.where(allowed, jnp.exp(scores - log_total[:, :, None]), 0.0)
        rounded = prob_rows.astype(jnp.bfloat16)
        remainder = (prob_rows - rounded.astype(jnp.float32)).astype(jnp.bfloat16)
        main_sum = main_sum + jnp.einsum(
            "hqk,khd->qhd", rounded, pieces[1], preferred_element_type=jnp.float32
        )
        extra_sum = extra_sum + jnp.einsum(
            "hqk,khd->qhd", remainder, pieces[1], preferred_element_type=jnp.float32
        )
        return (main_sum, extra_sum)

    zeros_out = jnp.zeros((query_rows, heads_part, HD), jnp.float32)
    main_sum, extra_sum = sweep_keys(value_step, (zeros_out, zeros_out))
    exact_out = main_sum + extra_sum
    attended_all = gather_query(main_sum.astype(jnp.bfloat16).reshape(query_rows, heads_part * HD))
    attn_out = sum_rows(jnp.dot(attended_all, w_out, preferred_element_type=jnp.float32))
    middle = stream_float + attn_out
    middle_square = sum_width(jnp.sum(middle * middle, axis=1))
    inv_ffn = lax.rsqrt(middle_square / D + EPS)
    unit_ffn = middle * inv_ffn[:, None]
    gain_ffn = norm_ffn.astype(jnp.float32)
    normed2_all = gather_rows((unit_ffn * gain_ffn).astype(jnp.bfloat16))
    slot_of, slot_token, slot_weight, slot_used = dispatch(routes, route_weights, E, CAPACITY)
    picked_grid = (normed2_all[slot_token] * slot_used[:, None].astype(jnp.bfloat16)).reshape(
        E, CAPACITY, width_part
    )
    gate_part = jnp.einsum(
        "ecd,edf->ecf", picked_grid, w_gate, preferred_element_type=jnp.float32
    ).reshape(E * CAPACITY, -1)
    up_part = jnp.einsum(
        "ecd,edf->ecf", picked_grid, w_up, preferred_element_type=jnp.float32
    ).reshape(E * CAPACITY, -1)
    sgate_part = jnp.dot(normed2_all, shared_gate, preferred_element_type=jnp.float32)
    sup_part = jnp.dot(normed2_all, shared_up, preferred_element_type=jnp.float32)
    logit_part = jnp.dot(normed2_all, shared_router, preferred_element_type=jnp.float32)
    gate_sum, up_sum, sgate_sum, sup_sum, gate_logit = (
        lax.psum_scatter(gate_part, "gy", scatter_dimension=0, tiled=True),
        lax.psum_scatter(up_part, "gy", scatter_dimension=0, tiled=True),
        lax.psum_scatter(sgate_part, "gy", scatter_dimension=0, tiled=True),
        lax.psum_scatter(sup_part, "gy", scatter_dimension=0, tiled=True),
        lax.psum_scatter(logit_part, "gy", scatter_dimension=0, tiled=True),
    )
    gate_act, gate_slope = silu_parts(gate_sum)
    hidden = (gate_act * up_sum).astype(jnp.bfloat16)
    mixer = jax.nn.sigmoid(gate_logit)
    sgate_act, sgate_slope = silu_parts(sgate_sum)
    shared_hidden = (mixer[:, None] * sgate_act * sup_sum).astype(jnp.bfloat16)
    hidden_all, shared_all = (
        lax.all_gather(hidden, "gy", axis=0, tiled=True),
        lax.all_gather(shared_hidden, "gy", axis=0, tiled=True),
    )
    hidden_grid = hidden_all.reshape(E, CAPACITY, -1)
    expert_out = jnp.einsum(
        "ecf,efd->ecd", hidden_grid, w_down, preferred_element_type=jnp.float32
    ).reshape(E * CAPACITY, width_part)
    routed = jnp.sum(
        expert_out[slot_of].reshape(SLOTS, TOPK, width_part) * route_weights[:, :, None], axis=1
    )
    branch = sum_rows(routed + jnp.dot(shared_all, shared_down, preferred_element_type=jnp.float32))
    result = middle + branch
    valid_col = local_valid[:, None]
    row_squares = sum_width(
        jnp.stack(
            [
                jnp.sum(result * result, axis=1),
                jnp.sum(attn_out * attn_out, axis=1),
                jnp.sum(branch * branch, axis=1),
            ]
        )
    )
    squares = jnp.stack(
        [
            jnp.sum(local_valid * middle_square),
            jnp.sum(local_valid * row_squares[0]),
            jnp.sum(local_valid * row_squares[1]),
            jnp.sum(local_valid * row_squares[2]),
            jnp.sum(local_valid) * D,
        ]
    )
    masked = cotangent * valid_col.astype(jnp.bfloat16)
    upstream = gather_rows(masked)
    slot_grid = (
        (upstream[slot_token].astype(jnp.float32) * slot_weight[:, None])
        .astype(jnp.bfloat16)
        .reshape(E, CAPACITY, width_part)
    )
    grad_w_down = jnp.einsum(
        "ecf,ecd->efd", hidden_grid, slot_grid, preferred_element_type=jnp.float32
    )
    grad_shared_down = jnp.einsum(
        "tf,td->fd", shared_all, upstream, preferred_element_type=jnp.float32
    )
    hidden_part = jnp.einsum(
        "ecd,efd->ecf", slot_grid, w_down, preferred_element_type=jnp.float32
    ).reshape(E * CAPACITY, -1)
    shared_part = jnp.einsum("td,fd->tf", upstream, shared_down, preferred_element_type=jnp.float32)
    hidden_grad, shared_grad = (
        lax.psum_scatter(hidden_part, "gy", scatter_dimension=0, tiled=True),
        lax.psum_scatter(shared_part, "gy", scatter_dimension=0, tiled=True),
    )
    gate_grad = (hidden_grad * up_sum * gate_slope).astype(jnp.bfloat16)
    up_grad = (hidden_grad * gate_act).astype(jnp.bfloat16)
    sgate_grad = (shared_grad * mixer[:, None] * sup_sum * sgate_slope).astype(jnp.bfloat16)
    sup_grad = (shared_grad * mixer[:, None] * sgate_act).astype(jnp.bfloat16)
    logit_grad = jnp.sum(shared_grad * sgate_act * sup_sum, axis=1) * mixer * (1.0 - mixer)
    gate_all, up_all, sgate_all, sup_all = (
        lax.all_gather(gate_grad, "gy", axis=0, tiled=True),
        lax.all_gather(up_grad, "gy", axis=0, tiled=True),
        lax.all_gather(sgate_grad, "gy", axis=0, tiled=True),
        lax.all_gather(sup_grad, "gy", axis=0, tiled=True),
    )
    logit_all = lax.all_gather(logit_grad, "gy", axis=0, tiled=True)
    gate_grid = gate_all.reshape(E, CAPACITY, -1)
    up_grid = up_all.reshape(E, CAPACITY, -1)
    grad_w_gate = jnp.einsum(
        "ecd,ecf->edf", picked_grid, gate_grid, preferred_element_type=jnp.float32
    )
    grad_w_up = jnp.einsum("ecd,ecf->edf", picked_grid, up_grid, preferred_element_type=jnp.float32)
    picked_grad = (
        jnp.einsum("ecf,edf->ecd", gate_grid, w_gate, preferred_element_type=jnp.float32)
        + jnp.einsum("ecf,edf->ecd", up_grid, w_up, preferred_element_type=jnp.float32)
    ).reshape(E * CAPACITY, width_part)
    grad_shared_gate = jnp.einsum(
        "td,tf->df", normed2_all, sgate_all, preferred_element_type=jnp.float32
    )
    grad_shared_up = jnp.einsum(
        "td,tf->df", normed2_all, sup_all, preferred_element_type=jnp.float32
    )
    router_part = jnp.dot(
        logit_all, normed2_all.astype(jnp.float32), precision=lax.Precision.HIGHEST
    )
    normed2_grad = (
        jnp.sum(picked_grad[slot_of].reshape(SLOTS, TOPK, width_part), axis=1)
        + jnp.einsum("tf,df->td", sgate_all, shared_gate, preferred_element_type=jnp.float32)
        + jnp.einsum("tf,df->td", sup_all, shared_up, preferred_element_type=jnp.float32)
        + logit_all[:, None] * shared_router.astype(jnp.float32)[None, :]
    )
    ffn_grad = sum_rows(normed2_grad)
    gain_ffn_part = jnp.sum(ffn_grad * unit_ffn, axis=0)
    scaled_ffn = ffn_grad * gain_ffn
    middle_grad = masked.astype(jnp.float32) + inv_ffn[:, None] * (
        scaled_ffn - unit_ffn * sum_width(jnp.sum(scaled_ffn * unit_ffn, axis=1))[:, None] / D
    )
    attn_grad_all = gather_rows(middle_grad.astype(jnp.bfloat16))
    grad_w_out = jnp.einsum(
        "tc,td->cd", attended_all, attn_grad_all, preferred_element_type=jnp.float32
    )
    out_grad = (
        sum_query(jnp.einsum("td,cd->tc", attn_grad_all, w_out, preferred_element_type=jnp.float32))
        .astype(jnp.bfloat16)
        .reshape(query_rows, heads_part, HD)
    )
    row_delta = jnp.transpose(jnp.sum(out_grad.astype(jnp.float32) * exact_out, axis=2))

    def back_step(running, pieces, offset):
        query_grad, key_grad, value_grad = running
        key_part, value_part = pieces
        row_count = key_part.shape[0]
        scores, allowed = scores_for(key_part, offset)
        prob_rows = jnp.where(allowed, jnp.exp(scores - log_total[:, :, None]), 0.0)
        value_piece = jnp.einsum(
            "hqk,qhd->khd",
            prob_rows.astype(jnp.bfloat16),
            out_grad,
            preferred_element_type=jnp.float32,
        )
        prob_grad = jnp.einsum(
            "qhd,khd->hqk", out_grad, value_part, preferred_element_type=jnp.float32
        )
        score_grad = (prob_rows * (prob_grad - row_delta[:, :, None])).astype(jnp.bfloat16)
        query_grad = (
            query_grad
            + jnp.einsum("hqk,khd->qhd", score_grad, key_part, preferred_element_type=jnp.float32)
            * score_scale
        )
        key_piece = (
            jnp.einsum("hqk,qhd->khd", score_grad, queries, preferred_element_type=jnp.float32)
            * score_scale
        )
        key_grad = lax.dynamic_update_slice_in_dim(
            key_grad,
            lax.dynamic_slice_in_dim(key_grad, offset, row_count, 0) + key_piece,
            offset,
            0,
        )
        value_grad = lax.dynamic_update_slice_in_dim(
            value_grad,
            lax.dynamic_slice_in_dim(value_grad, offset, row_count, 0) + value_piece,
            offset,
            0,
        )
        return (query_grad, key_grad, value_grad)

    zeros_all = jnp.zeros((SLOTS, heads_part, HD), jnp.float32)
    query_grad, key_grad, value_grad = sweep_keys(back_step, (zeros_out, zeros_all, zeros_all))
    pair_grad = sum_query(jnp.concatenate([key_grad, value_grad], axis=2))
    mixed_grad = jnp.concatenate(
        [
            rotate_back(query_grad, cos_table, sin_table),
            rotate_back(pair_grad[..., :HD], cos_table, sin_table),
            pair_grad[..., HD:],
        ],
        axis=2,
    ).astype(jnp.bfloat16)
    mixed_all = gather_query(mixed_grad)
    grad_qkv_bias = jnp.sum(mixed_all.astype(jnp.float32), axis=0)
    grad_w_qkv = jnp.einsum(
        "td,thc->dhc", normed_all, mixed_all, preferred_element_type=jnp.float32
    )
    attn_norm_grad = sum_rows(
        jnp.einsum("thc,dhc->td", mixed_all, w_qkv, preferred_element_type=jnp.float32)
    )
    gain_attn_part = jnp.sum(attn_norm_grad * unit_attn, axis=0)
    scaled_attn = attn_norm_grad * gain_attn
    grad_stream = middle_grad + inv_attn[:, None] * (
        scaled_attn - unit_attn * sum_width(jnp.sum(scaled_attn * unit_attn, axis=1))[:, None] / D
    )
    (
        grad_w_qkv,
        grad_qkv_bias,
        grad_w_out,
        grad_w_gate,
        grad_w_up,
        grad_w_down,
        grad_shared_gate,
        grad_shared_up,
        grad_shared_down,
    ) = (
        lax.psum(grad_w_qkv.astype(jnp.bfloat16), "dp").astype(jnp.float32),
        lax.psum(grad_qkv_bias.astype(jnp.bfloat16), "dp").astype(jnp.float32),
        lax.psum(grad_w_out.astype(jnp.bfloat16), "dp").astype(jnp.float32),
        lax.psum(grad_w_gate.astype(jnp.bfloat16), "dp").astype(jnp.float32),
        lax.psum(grad_w_up.astype(jnp.bfloat16), "dp").astype(jnp.float32),
        lax.psum(grad_w_down.astype(jnp.bfloat16), "dp").astype(jnp.float32),
        lax.psum(grad_shared_gate.astype(jnp.bfloat16), "dp").astype(jnp.float32),
        lax.psum(grad_shared_up.astype(jnp.bfloat16), "dp").astype(jnp.float32),
        lax.psum(grad_shared_down.astype(jnp.bfloat16), "dp").astype(jnp.float32),
    )
    small_grads = jnp.stack([gain_attn_part, gain_ffn_part, router_part])
    small_total, square_total = lax.psum((small_grads, squares), ("dp", "gx"))
    rms_stats = jnp.sqrt(square_total[:4] / square_total[4])
    return (
        result.astype(jnp.bfloat16),
        grad_stream,
        small_total[0],
        grad_w_qkv,
        grad_qkv_bias,
        grad_w_out,
        small_total[1],
        grad_w_gate,
        grad_w_up,
        grad_w_down,
        grad_shared_gate,
        grad_shared_up,
        grad_shared_down,
        small_total[2],
        rms_stats,
    )


def solution(mesh):
    placed = (
        P(("dp", "gx"), "gy"),
        P("dp"),
        P("dp", None),
        P("dp", None),
        P("gy"),
        P("gy", "gx", None),
        P("gx", None),
        P("gx", "gy"),
        P("gy"),
        P(None, "gy", "gx"),
        P(None, "gy", "gx"),
        P(None, "gx", "gy"),
        P("gy", "gx"),
        P("gy", "gx"),
        P("gx", "gy"),
        P("gy"),
        P(("dp", "gx"), "gy"),
    )
    return jax.shard_map(
        local,
        mesh=mesh,
        in_specs=placed,
        out_specs=(
            P(("dp", "gx"), "gy"),
            P(("dp", "gx"), "gy"),
            P("gy"),
            P("gy", "gx", None),
            P("gx", None),
            P("gx", "gy"),
            P("gy"),
            P(None, "gy", "gx"),
            P(None, "gy", "gx"),
            P(None, "gx", "gy"),
            P("gy", "gx"),
            P("gy", "gx"),
            P("gx", "gy"),
            P("gy"),
            P(),
        ),
        check_vma=False,
    )
```

profile of v0, /device:TPU:0, one launch (start us, length us, event | category | flops | bytes accessed | tf_op | source)
XLA Modules:
  0.0 5878.3 jit_solution(418064536253264099)
XLA Ops:
  19.4 117.3 %all-gather.16.cloned.1.call-done = bf16[3072,1024]{1,0:T(8,128)(2,1)} async-done(((bf16[768,1024]{1,0:T(8,128)(2,1)}), bf16[3072,1024]{1,0:T(8,128)(2,1)}) %all-gather.16.cloned.1.call-update) | async-done | bytes 6291472 | tf_op jit(solution)/shard_map/all_gather | solution.py:83
  158.1 204.5 %reduce-scatter.14.cloned.1.call-done = f32[1536,4,384]{2,0,1:T(8,128)} async-done(((f32[3072,4,384]{2,0,1:T(8,128)}), f32[1536,4,384]{2,0,1:T(8,128)}) %reduce-scatter.14.cloned.1.call-update) | async-done | bytes 9437200 | tf_op jit(solution)/shard_map/reduce_scatter | solution.py:95
  422.6 80.3 %while.41 = (s32[]{:T(128)}, f32[4,1536]{1,0:T(4,128)S(1)}, f32[4,1536]{1,0:T(4,128)S(1)}, s32[1536]{0:T(1024)S(1)}, s32[3]{0:T(128)S(1)}, /*index=5*/s32[3072]{...) while((s32[]{:T(128)}, f32[4,1536]{1,0:T(4,128)S(1)}, ...), condition=%wide.region_9.10_spmd.clone, body=%wide.region_6.9_spmd.clone.sunk | while | flops 1665696256 | bytes 58030296 | solution.py:116
  503.0 151.8 %while.42 = (s32[]{:T(128)}, f32[1536,4,128]{0,2,1:T(8,128)}, f32[1536,4,128]{0,2,1:T(8,128)}, bf16[3,1024,4,128]{3,1,0,2:T(8,128)(2,1)}, s32[1536]{0:T(1024)S(1...) while((s32[]{:T(128)}, f32[1536,4,128]{0,2,1:T(8,128)}, ...), condition=%wide.region_11.12_spmd.clone, body=%wide.region_10.11_spmd.clone.sunk | while | flops 4896328192 | bytes 121174304 | solution.py:116
  717.8 207.9 %reduce-scatter.16.cloned.1.call-done = f32[768,1024]{1,0:T(8,128)} async-done(((f32[3072,1024]{1,0:T(8,128)}), f32[768,1024]{1,0:T(8,128)}) %reduce-scatter.16.cloned.1.call-update) | async-done | bytes 3145744 | tf_op jit(solution)/shard_map/reduce_scatter | solution.py:87
  940.3 104.0 %all-gather.30.cloned.1.call-done = bf16[3072,1024]{1,0:T(8,128)(2,1)} async-done(((bf16[768,1024]{1,0:T(8,128)(2,1)}), bf16[3072,1024]{1,0:T(8,128)(2,1)}) %all-gather.30.cloned.1.call-update) | async-done | bytes 6291472 | tf_op jit(solution)/shard_map/all_gather | solution.py:83
  1061.1 99.0 %all-gather.24.cloned.1.call-done = bf16[3072,1024]{1,0:T(8,128)(2,1)} async-done(((bf16[768,1024]{1,0:T(8,128)(2,1)}), bf16[3072,1024]{1,0:T(8,128)(2,1)}) %all-gather.24.cloned.1.call-update) | async-done | bytes 6291472 | tf_op jit(solution)/shard_map/all_gather | solution.py:83
  1224.4 45.4 scatter_custom_fusion.2
  1269.8 45.8 scatter_custom_fusion
  1315.7 94.1 %gather_fusion.2 = bf16[18432,1024]{1,0:T(8,128)(2,1)} fusion(bf16[3072,1024]{1,0:T(8,128)(2,1)} %all-gather.30.cloned.1.call-done, s32[18432]{0:T(1024)S(1)} %fusion.137), kind=kCustom, calls=%fused_computation.2 | custom fusion | bytes 75571200 | tf_op jit(solution)/shard_map/gather | solution.py:290
  1456.8 45.4 scatter_custom_fusion.1
  1502.4 94.0 %gather_fusion = bf16[18432,1024]{1,0:T(8,128)(2,1)} fusion(bf16[3072,1024]{1,0:T(8,128)(2,1)} %all-gather.24.cloned.1.call-done, s32[18432]{0:T(1024)S(1)} %fusion.137), kind=kCustom, calls=%fused_computation | custom fusion | bytes 75571200 | tf_op jit(solution)/shard_map/gather | solution.py:231
  1705.4 46.2 reduce-scatter.22.cloned.1.call-done
  1778.8 262.8 %reduce-scatter.28.cloned.1.call-done = f32[9216,352]{0,1:T(8,128)} async-done(((f32[18432,352]{0,1:T(8,128)}), f32[9216,352]{0,1:T(8,128)}) %reduce-scatter.28.cloned.1.call-update) | async-done | bytes 12976144 | tf_op jit(solution)/shard_map/reduce_scatter | solution.py:305
  2041.5 290.2 %reduce-scatter.20.cloned.1.call-done = f32[9216,352]{0,1:T(8,128)} async-done(((f32[18432,352]{0,1:T(8,128)}), f32[9216,352]{0,1:T(8,128)}) %reduce-scatter.20.cloned.1.call-update) | async-done | bytes 12976144 | tf_op jit(solution)/shard_map/reduce_scatter | solution.py:245
  2331.7 290.0 %reduce-scatter.18.cloned.1.call-done = f32[9216,352]{0,1:T(8,128)} async-done(((f32[18432,352]{0,1:T(8,128)}), f32[9216,352]{0,1:T(8,128)}) %reduce-scatter.18.cloned.1.call-update) | async-done | bytes 12976144 | tf_op jit(solution)/shard_map/reduce_scatter | solution.py:244
  2652.3 81.1 %all-gather.36.cloned.1.call-done = bf16[3072,1408]{1,0:T(8,128)(2,1)} async-done(((bf16[1536,1408]{1,0:T(8,128)(2,1)}), bf16[3072,1408]{1,0:T(8,128)(2,1)}) %all-gather.36.cloned.1.call-update) | async-done | bytes 8650768 | tf_op jit(solution)/shard_map/all_gather | solution.py:316
  2750.4 141.8 %all-gather.32.cloned.1.call-done = bf16[18432,352]{0,1:T(8,128)(2,1)} async-done(((bf16[9216,352]{0,1:T(8,128)(2,1)}), bf16[18432,352]{0,1:T(8,128)(2,1)}) %all-gather.32.cloned.1.call-update) | async-done | bytes 12976144 | tf_op jit(solution)/shard_map/all_gather | solution.py:314
  2931.1 119.9 %all-gather.34.cloned.1.call-done = bf16[18432,352]{0,1:T(8,128)(2,1)} async-done(((bf16[9216,352]{0,1:T(8,128)(2,1)}), bf16[18432,352]{0,1:T(8,128)(2,1)}) %all-gather.34.cloned.1.call-update) | async-done | bytes 12976144 | tf_op jit(solution)/shard_map/all_gather | solution.py:315
  3051.0 63.0 %convolution_add_fusion = f32[16,1152,1024]{2,1,0:T(8,128)} fusion(f32[16,1152,1024]{2,1,0:T(8,128)} %fusion.85, bf16[16,1024,352]{1,2,0:T(8,128)(2,1)} %param.33, bf16[44,16,8,1152]{3,2,1,0:T(8,128)(2,1)} %bitcast.283), kind=kOutput, calls=%fused_computation.77 | convolution fusion | flops 13306429440 | bytes 175505408 | tf_op jit(solution)/shard_map/ecf,edf->ecd/dot_general | solution.py:328
  3114.0 233.5 %gather_fusion.3 = f32[12288,1024]{1,0:T(8,128)} fusion(f32[18432,1024]{1,0:T(8,128)} %bitcast.13, s32[12288]{0:T(1024)S(1)} %broadcast_clamp_fusion), kind=kCustom, calls=%fused_computation.3 | custom fusion | bytes 100712448 | tf_op jit(solution)/shard_map/gather | solution.py:340
  3347.5 56.0 reshape.281
  3498.6 231.4 %gather_fusion.1 = f32[12288,1024]{1,0:T(8,128)} fusion(f32[18432,1024]{1,0:T(8,128)} %bitcast.10, s32[12288]{0:T(1024)S(1)} %broadcast_clamp_fusion), kind=kCustom, calls=%fused_computation.1 | custom fusion | bytes 100712448 | tf_op jit(solution)/shard_map/gather | solution.py:264
  3730.0 55.8 reshape.275
  3842.8 211.9 %reduce-scatter.26.cloned.1.call-done = f32[768,1024]{1,0:T(8,128)} async-done(((f32[3072,1024]{1,0:T(8,128)}), f32[768,1024]{1,0:T(8,128)}) %reduce-scatter.26.cloned.1.call-update) | async-done | bytes 3145744 | tf_op jit(solution)/shard_map/reduce_scatter | solution.py:87
  4070.3 116.5 %all-gather.40.cloned.1.call-done = bf16[3072,1024]{1,0:T(8,128)(2,1)} async-done(((bf16[768,1024]{1,0:T(8,128)(2,1)}), bf16[3072,1024]{1,0:T(8,128)(2,1)}) %all-gather.40.cloned.1.call-update) | async-done | bytes 6291472 | tf_op jit(solution)/shard_map/all_gather | solution.py:83
  4196.1 75.4 %reduce-scatter.34.cloned.1.call-done = f32[1536,512]{1,0:T(8,128)} async-done(((f32[3072,512]{1,0:T(8,128)}), f32[1536,512]{1,0:T(8,128)}) %reduce-scatter.34.cloned.1.call-update) | async-done | bytes 3145744 | tf_op jit(solution)/shard_map/reduce_scatter | solution.py:95
  4289.2 185.1 %while.43 = (s32[]{:T(128)}, f32[1536,4,128]{0,2,1:T(8,128)}, f32[3072,4,128]{2,0,1:T(8,128)}, f32[3072,4,128]{2,0,1:T(8,128)}, bf16[3,1024,4,128]{3,1,2,0:T(8,1...) while((s32[]{:T(128)}, f32[1536,4,128]{0,2,1:T(8,128)}, ...), condition=%wide.region_38.39_spmd.clone, body=%wide.region_37.38_spmd.clone.sunk | while | flops 8112048640 | bytes 203512160 | solution.py:116
  4531.1 98.0 %reduce-scatter.36.cloned.1.call-done = f32[1536,4,256]{2,0,1:T(8,128)} async-done(((f32[3072,4,256]{2,0,1:T(8,128)}), f32[1536,4,256]{2,0,1:T(8,128)}) %reduce-scatter.36.cloned.1.call-update) | async-done | bytes 6291472 | tf_op jit(solution)/shard_map/reduce_scatter | solution.py:95
  4816.4 756.3 %all-reduce.6.cloned.1.call-done = (bf16[1024,4,384]{2,0,1:T(8,128)(2,1)}, bf16[512,1024]{1,0:T(8,128)(2,1)}, bf16[16,1024,352]{1,2,0:T(8,128)(2,1)}, bf16[16,10...) async-done(((bf16[1024,4,384]{2,0,1:T(8,128)(2,1)}, ...) | async-done | bytes 47448080 | tf_op jit(solution)/shard_map/psum | solution.py:436
  5623.8 163.3 %reduce-scatter.38.cloned.1.call-done = f32[768,1024]{1,0:T(8,128)} async-done(((f32[3072,1024]{1,0:T(8,128)}), f32[768,1024]{1,0:T(8,128)}) %reduce-scatter.38.cloned.1.call-update) | async-done | bytes 3145744 | tf_op jit(solution)/shard_map/reduce_scatter | solution.py:87
  5802.4 59.5 %all-reduce.1 = (f32[3,1024]{1,0:T(4,128)S(1)}, f32[5]{0:T(128)S(1)}) all-reduce(f32[3,1024]{1,0:T(4,128)S(1)} %pad_maximum_fusion.3, f32[5]{0:T(128)S(1)} %stack.55), channel_id=1, replica_groups=mesh['dp'=4,'gx'=4,'gy'=2] {'dp','gx'}, use_global_device_ids=true, to_apply=%region_45.46 | all-reduce | flops 3077 | bytes 24616 | tf_op jit(solution)/shard_map/psum | solution.py:447
  (459 shorter events, 1444.7 us)
Async XLA Ops:
  7.2 129.5 %all-gather.16.cloned.1.call-start = ((), (), s32[]{:S(2)}) async-start(), calls=%async_computation.13 | async-start | bytes 7864320 | tf_op jit(solution)/shard_map/all_gather | solution.py:83
  19.4 343.2 %reduce-scatter.14.cloned.1.call-start = ((), (), s32[]{:S(2)}) async-start(), calls=%async_computation.14 | async-start | bytes 28311552 | tf_op jit(solution)/shard_map/reduce_scatter | solution.py:95
  152.5 266.4 %all-gather.20.cloned.1.call-start = ((), (), s32[]{:S(2)}) async-start(), calls=%async_computation.16 | async-start | bytes 4718592 | tf_op jit(solution)/shard_map/all_gather | solution.py:187
  373.8 129.1 %all-gather.18.cloned.1.call-start = ((), (), s32[]{:S(2)}) async-start(), calls=%async_computation.15 | async-start | bytes 4718592 | tf_op jit(solution)/shard_map/all_gather | solution.py:188
  381.1 322.2 %all-gather.22.cloned.1.call-start = ((), (), s32[]{:S(2)}) async-start(), calls=%async_computation.17 | async-start | bytes 4718592 | tf_op jit(solution)/shard_map/all_gather | solution.py:99
  658.0 267.8 %reduce-scatter.16.cloned.1.call-start = ((), (), s32[]{:S(2)}) async-start(), calls=%async_computation.18 | async-start | bytes 15728640 | tf_op jit(solution)/shard_map/reduce_scatter | solution.py:87
  713.7 330.6 %all-gather.30.cloned.1.call-start = ((), (), s32[]{:S(2)}) async-start(), calls=%async_computation.27 | async-start | bytes 7864320 | tf_op jit(solution)/shard_map/all_gather | solution.py:83
  717.8 442.3 %all-gather.24.cloned.1.call-start = ((), (), s32[]{:S(2)}) async-start(), calls=%async_computation.19 | async-start | bytes 7864320 | tf_op jit(solution)/shard_map/all_gather | solution.py:83
  940.3 765.1 %reduce-scatter.30.cloned.1.call-start = ((), (), s32[]{:S(2)}) async-start(), calls=%async_computation.31 | async-start | bytes 25952256 | tf_op jit(solution)/shard_map/reduce_scatter | solution.py:306
  1060.8 644.6 %reduce-scatter.24.cloned.1.call-start = ((), (), s32[]{:S(2)}) async-start(), calls=%async_computation.24 | async-start | bytes 25952256 | tf_op jit(solution)/shard_map/reduce_scatter | solution.py:247
  1176.5 575.0 %reduce-scatter.22.cloned.1.call-start = ((), (), s32[]{:S(2)}) async-start(), calls=%async_computation.23 | async-start | bytes 25952256 | tf_op jit(solution)/shard_map/reduce_scatter | solution.py:246
  1193.1 848.4 %reduce-scatter.28.cloned.1.call-start = ((), (), s32[]{:S(2)}) async-start(), calls=%async_computation.28 | async-start | bytes 38928384 | tf_op jit(solution)/shard_map/reduce_scatter | solution.py:305
  1456.8 875.0 %reduce-scatter.20.cloned.1.call-start = ((), (), s32[]{:S(2)}) async-start(), calls=%async_computation.21 | async-start | bytes 38928384 | tf_op jit(solution)/shard_map/reduce_scatter | solution.py:245
  1643.4 978.3 %reduce-scatter.18.cloned.1.call-start = ((), (), s32[]{:S(2)}) async-start(), calls=%async_computation.20 | async-start | bytes 38928384 | tf_op jit(solution)/shard_map/reduce_scatter | solution.py:244
  1690.6 1042.7 %all-gather.36.cloned.1.call-start = ((), (), s32[]{:S(2)}) async-start(), calls=%async_computation.32 | async-start | bytes 12976128 | tf_op jit(solution)/shard_map/all_gather | solution.py:316
  1778.7 1113.5 %all-gather.32.cloned.1.call-start = ((), (), s32[]{:S(2)}) async-start(), calls=%async_computation.29 | async-start | bytes 19464192 | tf_op jit(solution)/shard_map/all_gather | solution.py:314
  2645.1 406.0 %all-gather.34.cloned.1.call-start = ((), (), s32[]{:S(2)}) async-start(), calls=%async_computation.30 | async-start | bytes 19464192 | tf_op jit(solution)/shard_map/all_gather | solution.py:315
  2645.7 793.6 %all-gather.38.cloned.1.call-start = ((), (), s32[]{:S(2)}) async-start(), calls=%async_computation.33 | async-start | bytes 12976128 | tf_op jit(solution)/shard_map/all_gather | solution.py:317
  2646.2 815.4 %all-gather.26.cloned.1.call-start = ((), (), s32[]{:S(2)}) async-start(), calls=%async_computation.22 | async-start | bytes 19464192 | tf_op jit(solution)/shard_map/all_gather | solution.py:256
  2647.0 1177.5 %all-gather.28.cloned.1.call-start = ((), (), s32[]{:S(2)}) async-start(), calls=%async_computation.25 | async-start | bytes 12976128 | tf_op jit(solution)/shard_map/all_gather | solution.py:257
  2652.2 1190.5 %reduce-scatter.32.cloned.1.call-start = ((), (), s32[]{:S(2)}) async-start(), calls=%async_computation.34 | async-start | bytes 15728640 | tf_op jit(solution)/shard_map/reduce_scatter | solution.py:87
  3461.5 593.1 %reduce-scatter.26.cloned.1.call-start = ((), (), s32[]{:S(2)}) async-start(), calls=%async_computation.26 | async-start | bytes 15728640 | tf_op jit(solution)/shard_map/reduce_scatter | solution.py:87
  3842.7 344.1 %all-gather.40.cloned.1.call-start = ((), (), s32[]{:S(2)}) async-start(), calls=%async_computation.35 | async-start | bytes 7864320 | tf_op jit(solution)/shard_map/all_gather | solution.py:83
  4070.2 201.2 %reduce-scatter.34.cloned.1.call-start = ((), (), s32[]{:S(2)}) async-start(), calls=%async_computation.36 | async-start | bytes 9437184 | tf_op jit(solution)/shard_map/reduce_scatter | solution.py:95
  4196.0 433.1 %reduce-scatter.36.cloned.1.call-start = ((), (), s32[]{:S(2)}) async-start(), calls=%async_computation.37 | async-start | bytes 18874368 | tf_op jit(solution)/shard_map/reduce_scatter | solution.py:95
  4484.5 281.8 %all-gather.42.cloned.1.call-start = ((), (), s32[]{:S(2)}) async-start(), calls=%async_computation.38 | async-start | bytes 14155776 | tf_op jit(solution)/shard_map/all_gather | solution.py:99
  4648.9 923.8 %all-reduce.6.cloned.1.call-start = ((), (), s32[]{:S(2)}) async-start(), calls=%async_computation.40 | async-start | bytes 94896128 | tf_op jit(solution)/shard_map/psum | solution.py:436
  4782.3 1004.8 %reduce-scatter.38.cloned.1.call-start = ((), (), s32[]{:S(2)}) async-start(), calls=%async_computation.39 | async-start | bytes 15728640 | tf_op jit(solution)/shard_map/reduce_scatter | solution.py:87
  5615.4 248.8 %copy-start.24 = (f32[1024]{0:T(1024)S(1)}, f32[1024]{0:T(1024)}, u32[]{:S(2)}) copy-start(f32[1024]{0:T(1024)} %copy-done.22) | copy-start | bytes 12292
  5615.4 248.8 %copy-start.27 = (f32[768]{0:T(1024)S(1)}, f32[768]{0:T(1024)}, u32[]{:S(2)}) copy-start(f32[768]{0:T(1024)} %copy-done.25) | copy-start | bytes 9220
  5615.4 248.8 %copy-start.38 = (f32[768]{0:T(1024)S(1)}, f32[768]{0:T(1024)}, u32[]{:S(2)}) copy-start(f32[768]{0:T(1024)} %copy-done.37) | copy-start | bytes 9220
  5615.5 248.8 %copy-start.45 = (bf16[768]{0:T(1024)(128)(2,1)S(1)}, bf16[768]{0:T(1024)(128)(2,1)}, u32[]{:S(2)}) copy-start(bf16[768]{0:T(1024)(128)(2,1)} %copy-done.43) | copy-start | bytes 4612
  (79 other events, 3633.7 us)
Sparse Core Ops, SparseCore 0:
  19.5 117.1 all-gather.15
  152.6 209.9 reduce-scatter.13
  373.9 44.9 all-gather.19
  420.9 44.9 all-gather.17
  658.1 45.1 all-gather.21
  713.9 211.8 reduce-scatter.15
  927.9 116.3 all-gather.29
  1046.5 113.5 all-gather.23
  1163.0 192.9 reduce-scatter.29
  1358.7 194.7 reduce-scatter.23
  1556.4 195.0 reduce-scatter.21
  1753.7 287.7 reduce-scatter.27
  2044.0 287.7 reduce-scatter.19
  2333.9 287.7 reduce-scatter.17
  2623.8 109.5 all-gather.35
  2735.4 156.7 all-gather.31
  2894.2 156.7 all-gather.33
  3053.1 109.3 all-gather.37
  3164.1 156.7 all-gather.25
  3323.0 109.3 all-gather.27
  3461.7 211.8 reduce-scatter.31
  3842.8 211.7 reduce-scatter.25
  4070.4 116.3 all-gather.39
  4196.2 75.2 reduce-scatter.33
  4484.6 144.4 reduce-scatter.35
  4649.0 117.2 all-gather.41
  4782.4 790.2 all-reduce.5
  5575.1 211.8 reduce-scatter.37
where the time goes:
time: 5900 us; the launch traced here: 5880 us
  waiting for transfers between devices  3500 us (59%)
  local copies, waits for them, and re-layouts  1050 us (18%)
  matrix products  881 us (15%)
  other arithmetic  320 us (5%)
  blocking collectives  104 us (2%)
    psum x1, waiting for transfers between devices, local(): lax.psum(grad_w_qkv.astype(jnp.bfloat16), 'dp').astype(jnp.float32)  756 us
    reduce_scatter x4, waiting for transfers between devices, sum_rows(): return lax.psum_scatter(values, 'gx', scatter_dimension=0, tiled=True)  583 us
    all_gather x4, waiting for transfers between devices, gather_rows(): return lax.all_gather(values, 'gx', axis=0, tiled=True)  437 us
    reduce_scatter x3, waiting for transfers between devices, sum_query(): return lax.psum_scatter(values, 'gy', scatter_dimension=0, tiled=True)  378 us
    reduce_scatter x1, waiting for transfers between devices, local(): lax.psum_scatter(up_part, 'gy', scatter_dimension=0, tiled=True)  290 us
    reduce_scatter x1, waiting for transfers between devices, local(): lax.psum_scatter(gate_part, 'gy', scatter_dimension=0, tiled=True)  290 us
    reduce_scatter x1, waiting for transfers between devices, local(): lax.psum_scatter(hidden_part, 'gy', scatter_dimension=0, tiled=True)  263 us
    gather x1, local copies, waits for them, and re-layouts, local(): picked_grad[slot_of].reshape(SLOTS, TOPK, width_part)  234 us
  transfers between devices with their start and end apart: 28, of which 21 were waited for; matrix products, arithmetic and copies ran while one was open for 30% of the time, Pallas kernels for 0%

commit v1 on v0

v1 whole, which is shorter than its diff:
```python
import functools

import jax
import jax.numpy as jnp
from jax import lax
from jax.experimental import pallas as pl
from jax.experimental.pallas import tpu as pltpu
from jax.sharding import PartitionSpec as P

HD = 128
E = 16
TM = 256
PIECE = 16
PAIR = 2

EPS = 1e-06
THETA = 1000000.0
NEG = -1e30
LOW = -1e20
LOG2E = 1.4426950408889634
F32 = jnp.float32
BF16 = jnp.bfloat16
LIMIT = 60 * 2**20


def dot(a, b, dims=((1,), (0,))):
    return lax.dot_general(a, b, (dims, ((), ())), preferred_element_type=F32)


def params(n=1):
    return pltpu.CompilerParams(
        dimension_semantics=("arbitrary",) * n, vmem_limit_bytes=LIMIT
    )


def cost(flops, nbytes):
    return pl.CostEstimate(flops=int(flops), bytes_accessed=int(nbytes), transcendentals=0)


def fixed(shape):
    zeros = (0,) * len(shape)
    return pl.BlockSpec(shape, lambda *_: zeros, pipeline_mode=pl.Buffered(1))


def turn(values, cos, sin):
    return values * cos + pltpu.roll(values, HD // 2, 1) * sin


def qkv_body(n1, w, bias, cos, sin, q_out, kv_out):
    mixed = dot(n1[...], w[...]) + bias[0].astype(F32)
    q_out[...] = turn(mixed[:, :HD], cos[...], sin[...]).astype(BF16)
    kv_out[:, :HD] = turn(mixed[:, HD : 2 * HD], cos[...], sin[...]).astype(BF16)
    kv_out[:, HD:] = mixed[:, 2 * HD :].astype(BF16)


def project_qkv(n1, w, bias, cos, sin):
    rows, depth = n1.shape
    heads = bias.shape[0]
    return pl.pallas_call(
        qkv_body,
        grid=(heads,),
        in_specs=[
            fixed((rows, depth)),
            pl.BlockSpec((depth, 3 * HD), lambda h: (0, h)),
            pl.BlockSpec((1, 1, 3 * HD), lambda h: (h, 0, 0)),
            fixed((rows, HD)),
            fixed((rows, HD)),
        ],
        out_specs=[
            pl.BlockSpec((rows, HD), lambda h: (0, h)),
            pl.BlockSpec((rows, 2 * HD), lambda h: (0, h)),
        ],
        out_shape=[
            jax.ShapeDtypeStruct((rows, heads * HD), BF16),
            jax.ShapeDtypeStruct((rows, heads * 2 * HD), BF16),
        ],
        compiler_params=params(),
        cost_estimate=cost(2 * rows * depth * heads * 3 * HD, 4 * rows * depth),
        name="project_qkv",
    )(n1, w, bias[:, None, :], cos, sin)


def first_of(place, ends, count):
    start = jnp.zeros_like(place)
    for n in range(count):
        start = jnp.where(place >= ends[n], ends[n], start)
    return start


def pair_visible(q_start, k_start, size, ends, count):
    begin = jnp.int32(0)
    for n in range(count):
        begin = jnp.where(q_start >= ends[n], ends[n], begin)
    return (k_start <= q_start + size - 1) & (k_start + size - 1 >= begin)


def allowed_mask(q_start, k_start, size, ends, count):
    q_place = q_start + lax.broadcasted_iota(jnp.int32, (size, 1), 0)
    k_place = k_start + lax.broadcasted_iota(jnp.int32, (1, size), 1)
    return (k_place <= q_place) & (k_place >= first_of(q_place, ends, count))


def attend_body(dims, meta, q, kv_own, kv_rem, o_out, exact_out, lse_out, top, main, extra):
    size, blocks, parts, count, pair = dims
    scale = HD ** (-0.5) * LOG2E
    j = pl.program_id(1)
    part = meta[count]
    span = size * parts
    ones = jnp.ones((size, HD), BF16)
    q_start = j * span + part * size
    top[...] = jnp.full_like(top, LOW)
    main[...] = jnp.zeros_like(main)
    extra[...] = jnp.zeros_like(extra)
    q_place = q_start + lax.broadcasted_iota(jnp.int32, (size, 1), 0)
    begin = first_of(q_place, meta, count)
    for shift in range(parts):
        owner = lax.rem(part + shift, parts)

        @pl.loop(0, j + 1)
        def _(jj):
            k_start = jj * span + owner * size

            @pl.when(pair_visible(q_start, k_start, size, meta, count))
            def _():
                if shift == 0:
                    there, kv = pl.ds(jj * size, size), kv_own
                else:
                    there, kv = pl.ds(((shift - 1) * blocks + jj) * size, size), kv_rem
                k_place = k_start + lax.broadcasted_iota(jnp.int32, (1, size), 1)
                allowed = (k_place <= q_place) & (k_place >= begin)
                for u in range(pair):
                    keys = kv[there, 2 * u * HD : (2 * u + 1) * HD]
                    values = kv[there, (2 * u + 1) * HD : (2 * u + 2) * HD]
                    s = dot(q[:, u * HD : (u + 1) * HD], keys, ((1,), (1,))) * scale
                    s = jnp.where(allowed, s, NEG)
                    old = top[u]
                    new = jnp.maximum(old, jnp.max(s, axis=1, keepdims=True))
                    p = jnp.exp2(s - new[:, :1])
                    fade = jnp.exp2(old - new)
                    fade = jnp.concatenate([fade, fade], axis=1)
                    coarse = p.astype(BF16)
                    fine = (p - coarse.astype(F32)).astype(BF16)
                    values = jnp.concatenate([values, ones], axis=1)
                    main[u] = main[u] * fade + dot(coarse, values)
                    extra[u] = extra[u] * fade + dot(fine, values)
                    top[u] = new

    for u in range(pair):
        here = slice(u * HD, (u + 1) * HD)
        exact = main[u] + extra[u]
        share = 1.0 / exact[:, HD:]
        o_out[:, here] = (main[u, :, :HD] * share).astype(BF16)
        exact_out[:, here] = exact[:, :HD] * share
        lse_out[:, here] = top[u] + jnp.log2(exact[:, HD:])


def attend(meta, q, kv_own, kv_rem, size, parts, count):
    rows, width = q.shape
    heads, blocks = width // HD, rows // size
    pair = next(n for n in (PAIR, 2, 1) if heads % n == 0)
    block = pl.BlockSpec((size, pair * HD), lambda h, j, *_: (j, h))
    return pl.pallas_call(
        functools.partial(attend_body, (size, blocks, parts, count, pair)),
        grid_spec=pltpu.PrefetchScalarGridSpec(
            num_scalar_prefetch=1,
            grid=(heads // pair, blocks),
            in_specs=[
                block,
                pl.BlockSpec((rows, 2 * pair * HD), lambda h, j, *_: (0, h)),
                pl.BlockSpec((rows * (parts - 1), 2 * pair * HD), lambda h, j, *_: (0, h)),
            ],
            out_specs=[block, block, block],
            scratch_shapes=[
                pltpu.VMEM((pair, size, HD), F32),
                pltpu.VMEM((pair, size, 2 * HD), F32),
                pltpu.VMEM((pair, size, 2 * HD), F32),
            ],
        ),
        out_shape=[
            jax.ShapeDtypeStruct((rows, width), BF16),
            jax.ShapeDtypeStruct((rows, width), F32),
            jax.ShapeDtypeStruct((rows, width), F32),
        ],
        compiler_params=params(2),
        cost_estimate=cost(12 * rows * rows * width, 30 * rows * width),
        name="attend",
    )(meta, q, kv_own, kv_rem)


def attend_back_body(
    dims, meta, q, kv_own, kv_rem, d_o, exact, lse, cos, sin, dq_out, own_out, rem_out, dq_sum, kv_sum
):
    size, blocks, parts, count = dims
    scale = HD ** (-0.5)
    part = meta[count]
    span = size * parts
    kv_sum[...] = jnp.zeros_like(kv_sum)

    @pl.loop(0, blocks)
    def _(j):
        q_start = j * span + part * size
        here = pl.ds(j * size, size)
        q_piece, do_piece = q[here, :], d_o[here, :]
        delta = jnp.sum(do_piece.astype(F32) * exact[here, :], axis=1, keepdims=True)
        level = lse[here, :][:, :1]
        dq_sum[...] = jnp.zeros_like(dq_sum)
        for shift in range(parts):
            owner = lax.rem(part + shift, parts)

            @pl.loop(0, j + 1)
            def _(jj):
                k_start = jj * span + owner * size

                @pl.when(pair_visible(q_start, k_start, size, meta, count))
                def _():
                    if shift == 0:
                        piece = kv_own[pl.ds(jj * size, size), :]
                    else:
                        piece = kv_rem[pl.ds(((shift - 1) * blocks + jj) * size, size), :]
                    there = pl.ds((shift * blocks + jj) * size, size)
                    allowed = allowed_mask(q_start, k_start, size, meta, count)
                    s = dot(q_piece, piece[:, :HD], ((1,), (1,))) * (scale * LOG2E)
                    p = jnp.where(allowed, jnp.exp2(s - level), 0.0)
                    dp = dot(do_piece, piece[:, HD:], ((1,), (1,)))
                    ds = (p * (dp - delta)).astype(BF16)
                    dq_sum[...] += dot(ds, piece[:, :HD])
                    kv_sum[there, :HD] += dot(ds, q_piece, ((0,), (0,)))
                    kv_sum[there, HD:] += dot(p.astype(BF16), do_piece, ((0,), (0,)))

        dq_out[here, :] = turn(dq_sum[...] * scale, cos[here, :], -sin[here, :]).astype(BF16)

    rows = blocks * size
    own_out[:, :HD] = kv_sum[:rows, :HD] * scale
    own_out[:, HD:] = kv_sum[:rows, HD:]
    rem_out[:, :HD] = (kv_sum[rows:, :HD] * scale).astype(BF16)
    rem_out[:, HD:] = kv_sum[rows:, HD:].astype(BF16)


def attend_back(meta, q, kv_own, kv_rem, d_o, exact, lse, cos, sin, size, parts, count):
    rows, width = q.shape
    heads, blocks = width // HD, rows // size
    narrow = pl.BlockSpec((rows, HD), lambda h, *_: (0, h))
    wide = pl.BlockSpec((rows, 2 * HD), lambda h, *_: (0, h))
    rest = pl.BlockSpec((rows * (parts - 1), 2 * HD), lambda h, *_: (0, h))
    return pl.pallas_call(
        functools.partial(attend_back_body, (size, blocks, parts, count)),
        grid_spec=pltpu.PrefetchScalarGridSpec(
            num_scalar_prefetch=1,
            grid=(heads,),
            in_specs=[narrow, wide, rest, narrow, narrow, narrow, fixed((rows, HD)), fixed((rows, HD))],
            out_specs=[narrow, wide, rest],
            scratch_shapes=[
                pltpu.VMEM((size, HD), F32),
                pltpu.VMEM((rows * parts, 2 * HD), F32),
            ],
        ),
        out_shape=[
            jax.ShapeDtypeStruct((rows, width), BF16),
            jax.ShapeDtypeStruct((rows, 2 * width), F32),
            jax.ShapeDtypeStruct((rows * (parts - 1), 2 * width), BF16),
        ],
        compiler_params=params(),
        cost_estimate=cost(20 * rows * rows * width, 40 * rows * width),
        name="attend_back",
    )(meta, q, kv_own, kv_rem, d_o, exact, lse, cos, sin)


def mix_body(arrived, dq, own, *refs):
    got, (cos, sin, out, bias_out) = refs[:arrived], refs[arrived:]
    total = own[...]
    for piece in got:
        total = total + piece[...].astype(F32)
    out[:, :HD] = dq[...]
    out[:, HD : 2 * HD] = turn(total[:, :HD], cos[...], -sin[...]).astype(BF16)
    out[:, 2 * HD :] = total[:, HD:].astype(BF16)
    bias_out[0] = jnp.sum(out[...].astype(F32), axis=0, keepdims=True)


def mix_back(dq, own, got, cos, sin):
    rows, width = dq.shape
    heads = width // HD
    wide = pl.BlockSpec((rows, 2 * HD), lambda h: (0, h))
    return pl.pallas_call(
        functools.partial(mix_body, len(got)),
        grid=(heads,),
        in_specs=[pl.BlockSpec((rows, HD), lambda h: (0, h)), wide]
        + [wide] * len(got)
        + [fixed((rows, HD)), fixed((rows, HD))],
        out_specs=[
            pl.BlockSpec((rows, 3 * HD), lambda h: (0, h)),
            pl.BlockSpec((1, 1, 3 * HD), lambda h: (h, 0, 0)),
        ],
        out_shape=[
            jax.ShapeDtypeStruct((rows, heads * 3 * HD), BF16),
            jax.ShapeDtypeStruct((heads, 1, 3 * HD), F32),
        ],
        compiler_params=params(),
        cost_estimate=cost(rows * width * 20, rows * width * 20),
        name="mix_back",
    )(dq, own, *got, cos, sin)


def plan_tiles(route_rows, weight_rows, block):
    rows, top = route_rows.shape
    blocks = rows // block
    per_tile = TM // PIECE
    room = (top * block + E * (PIECE - 1)) // PIECE
    number = (top * rows + E * blocks * (PIECE - 1) + E * TM) // TM
    experts = jnp.arange(E, dtype=jnp.int32)
    steps = jnp.arange(blocks, dtype=jnp.int32)
    match = route_rows[:, :, None] == experts
    spread = jnp.any(match, axis=1).T.reshape(E, blocks, block)
    order = jnp.arange(block, dtype=jnp.int32)
    before = (order[:, None] < order[None, :]).astype(BF16)
    rank = jnp.einsum("ebt,tu->ebu", spread.astype(BF16), before, preferred_element_type=F32)
    held = (jnp.sum(spread.astype(jnp.int32), axis=2) + PIECE - 1) // PIECE
    lower = (experts[:, None] < experts[None, :]).astype(jnp.int32)
    start = jnp.sum(lower[:, :, None] * held[:, None, :], axis=0)
    ahead = jnp.sum(
        jnp.where(steps[:, None] < steps[None, :], held[:, :, None], 0), axis=1
    )
    load = jnp.sum(held, axis=1)
    tiles = jnp.maximum((load + per_tile - 1) // per_tile, 1)
    begin = jnp.sum(lower * tiles[:, None], axis=0)
    spot = (rank.astype(jnp.int32) + start[:, :, None] * PIECE).reshape(E, rows).T
    spot = jnp.sum(jnp.where(match, spot[:, None, :], 0), axis=2)
    piece = jnp.arange(room, dtype=jnp.int32)
    inside = (piece[None, None, :] >= start[:, :, None]) & (
        piece[None, None, :] < (start + held)[:, :, None]
    )
    where_to = (begin[:, None] * per_tile + ahead - start)[:, :, None] + piece[None, None, :]
    where_to = jnp.sum(jnp.where(inside, where_to, 0), axis=0)
    halves = []
    for half in range(2):
        low, high = half * E // 2, (half + 1) * E // 2
        room_of = (top * rows + (high - low) * (blocks * (PIECE - 1) + TM)) // TM
        turn_in = jnp.arange(room_of, dtype=jnp.int32)
        from_tile = jnp.sum(tiles[:low])
        total = jnp.sum(tiles[low:high])
        place = from_tile + jnp.minimum(turn_in, total - 1)
        expert = jnp.sum((place[:, None] >= (begin + tiles)[None, :]).astype(jnp.int32), axis=1)
        pick = (expert[:, None] == experts[None, :]).astype(jnp.int32)
        turn_of = place - jnp.sum(pick * begin[None, :], axis=1)
        active = turn_in < total
        last = active & (turn_of == jnp.sum(pick * tiles[None, :], axis=1) - 1)
        limit = jnp.sum(pick * load[None, :], axis=1) * PIECE - turn_of * TM
        inner = turn_of[:, None] * per_tile + jnp.arange(per_tile, dtype=jnp.int32)[None, :]
        ahead_of = jnp.sum(pick[:, :, None] * ahead[None], axis=1)[:, None, :]
        held_of = jnp.sum(pick[:, :, None] * held[None], axis=1)[:, None, :]
        start_of = jnp.sum(pick[:, :, None] * start[None], axis=1)[:, None, :]
        inner = inner[:, :, None]
        inside = (inner >= ahead_of) & (inner < ahead_of + held_of)
        source = inner - ahead_of + start_of + (steps * room)[None, None, :]
        source = jnp.sum(jnp.where(inside, source, 0), axis=2)
        meta = jnp.stack(
            [
                expert,
                place,
                active.astype(jnp.int32),
                (active & (turn_of == 0)).astype(jnp.int32),
                last.astype(jnp.int32),
                limit,
            ]
        )
        halves.append((meta, source))
    spot = spot.reshape(blocks, block, top)
    weight = weight_rows.reshape(blocks, block, top)
    return dict(
        halves=halves,
        number=number,
        get=where_to,
        room=room,
        column=spot,
        line=jnp.swapaxes(spot, 1, 2),
        weight=weight,
        line_weight=jnp.swapaxes(weight, 1, 2),
    )


def send_out_body(dims, line, *refs):
    top, chunk, scaled = dims
    weight = refs[0] if scaled else None
    values, out, held = refs[-3:]
    rows, block = out.shape[1], values.shape[1]
    held[...] = values[0]

    @pl.loop(0, rows // chunk)
    def _(c):
        ids = lax.broadcasted_iota(jnp.int32, (chunk, block), 0) + c * chunk
        chosen = jnp.zeros((chunk, block), F32)
        level = jnp.zeros((chunk, block), F32)
        for r in range(top):
            hit = ids == line[0, r : r + 1, :]
            chosen = jnp.where(hit, 1.0, chosen)
            if scaled:
                level = jnp.where(hit, weight[0, r : r + 1, :], level)
        value = dot(chosen.astype(BF16), held[...])
        if scaled:
            value = value * jnp.sum(level, axis=1, keepdims=True)
        out[0, pl.ds(pl.multiple_of(c * chunk, chunk), chunk), :] = value.astype(BF16)


def send_out(plan, values, scaled):
    blocks, block, depth = values.shape
    top = plan["column"].shape[2]
    rows = plan["room"] * PIECE
    chunk = rows
    line = pl.BlockSpec((1, top, block), lambda b: (b, 0, 0))
    extra = [plan["line_weight"]] if scaled else []
    return pl.pallas_call(
        functools.partial(send_out_body, (top, chunk, scaled)),
        grid=(blocks,),
        in_specs=[line] * (1 + len(extra)) + [pl.BlockSpec((1, block, depth), lambda b: (b, 0, 0))],
        out_specs=pl.BlockSpec((1, rows, depth), lambda b: (b, 0, 0)),
        scratch_shapes=[pltpu.VMEM((block, depth), BF16)],
        out_shape=jax.ShapeDtypeStruct((blocks, rows, depth), BF16),
        compiler_params=params(),
        cost_estimate=cost(2 * blocks * rows * block * depth, 4 * blocks * rows * depth),
        name="send_out",
    )(plan["line"], *extra, values).reshape(blocks * rows, depth)


def bring_back_body(dims, get, column, *refs):
    blocks, top, room, weighted = dims
    weight = refs[0] if weighted else None
    packed, out, buf, sem = refs[-4:]
    b = pl.program_id(0)
    slot = lax.rem(b, 2)
    rows, block = buf.shape[1], out.shape[1]

    def fetch(which, into):
        @pl.loop(0, room)
        def _(i):
            pltpu.make_async_copy(
                packed.at[pl.ds(pl.multiple_of(get[which, i] * PIECE, PIECE), PIECE)],
                buf.at[into, pl.ds(pl.multiple_of(i * PIECE, PIECE), PIECE)],
                sem.at[into],
            ).start()

    @pl.when(b == 0)
    def _():
        fetch(b, slot)

    @pl.when(b < blocks - 1)
    def _():
        fetch(b + 1, 1 - slot)

    ids = lax.broadcasted_iota(jnp.int32, (block, rows), 1)
    chosen = jnp.zeros((block, rows), F32)
    for r in range(top):
        level = weight[0, :, r : r + 1] if weighted else 1.0
        chosen = jnp.where(ids == column[0, :, r : r + 1], level, chosen)
    pltpu.make_async_copy(packed.at[pl.ds(0, rows)], buf.at[slot], sem.at[slot]).wait()
    out[0] = dot(chosen.astype(BF16), buf[slot]).astype(BF16)


def bring_back(plan, packed, block, weighted):
    blocks, room = plan["get"].shape
    top = plan["column"].shape[2]
    depth = packed.shape[1]
    rows = room * PIECE
    column = pl.BlockSpec((1, block, top), lambda b, *_: (b, 0, 0))
    extra = [plan["weight"]] if weighted else []
    return pl.pallas_call(
        functools.partial(bring_back_body, (blocks, top, room, weighted)),
        grid_spec=pltpu.PrefetchScalarGridSpec(
            num_scalar_prefetch=1,
            grid=(blocks,),
            in_specs=[column] * (1 + len(extra)) + [pl.BlockSpec(memory_space=pl.ANY)],
            out_specs=pl.BlockSpec((1, block, depth), lambda b, *_: (b, 0, 0)),
            scratch_shapes=[pltpu.VMEM((2, rows, depth), BF16), pltpu.SemaphoreType.DMA((2,))],
        ),
        out_shape=jax.ShapeDtypeStruct((blocks, block, depth), BF16),
        compiler_params=params(),
        cost_estimate=cost(2 * blocks * rows * block * depth, 4 * blocks * rows * depth),
        name="bring_back",
    )(plan["get"], plan["column"], *extra, packed)


def experts_body(dims, meta, source, spot, x, d, gu_own, gu_rem, down_own, down_rem, *refs):
    cut, number, hidden, later = dims
    got, refs = (refs[:4], refs[6:]) if later else ((), refs)
    out, dx = refs[:2]
    results = refs[2:6]
    xs, ds, dgu = refs[6:9]
    totals, sem = refs[9:13], refs[13]
    i = pl.program_id(0)
    slot = lax.rem(i, 2)
    rows, cols = ((0,), (0,)), ((1,), (1,))

    def fetch(which, into):
        @pl.loop(0, TM // PIECE)
        def _(n):
            there = pl.ds(pl.multiple_of(source[which, n] * PIECE, PIECE), PIECE)
            here = pl.ds(pl.multiple_of(n * PIECE, PIECE), PIECE)
            pltpu.make_async_copy(x.at[there], xs.at[into, here], sem.at[0, into]).start()
            pltpu.make_async_copy(d.at[there], ds.at[into, here], sem.at[1, into]).start()

    @pl.when(i == 0)
    def _():
        fetch(i, slot)

    @pl.when((i < number - 1) & (meta[2, jnp.minimum(i + 1, number - 1)] == 1))
    def _():
        fetch(i + 1, 1 - slot)

    @pl.when(meta[3, i] == 1)
    def _():
        for total in totals:
            total[...] = jnp.zeros_like(total)

    @pl.when(meta[2, i] == 1)
    def _():
        pltpu.make_async_copy(x.at[pl.ds(0, TM)], xs.at[slot], sem.at[0, slot]).wait()
        pltpu.make_async_copy(d.at[pl.ds(0, TM)], ds.at[slot], sem.at[1, slot]).wait()
        limit = meta[5, i]

        @pl.when(limit < TM)
        def _():
            inside = lax.broadcasted_iota(jnp.int32, xs.shape[1:], 0) < limit
            for ref in (xs, ds):
                ref[slot] = jnp.where(inside, ref[slot], jnp.zeros(xs.shape[1:], BF16))

        x_own, x_rem = xs[slot, :, :cut], xs[slot, :, cut:]
        d_own, d_rem = ds[slot, :, :cut], ds[slot, :, cut:]
        both = dot(x_own, gu_own[0], cols) + dot(x_rem, gu_rem[0], cols)
        gate, up = both[:, :hidden], both[:, hidden:]
        d_hidden = dot(d_own, down_own[0], cols) + dot(d_rem, down_rem[0], cols)
        logistic = jax.nn.sigmoid(gate)
        act = gate * logistic
        h = (act * up).astype(BF16)
        dgu[:, :hidden] = (d_hidden * up * logistic * (1.0 + gate * (1.0 - logistic))).astype(BF16)
        dgu[:, hidden:] = (d_hidden * act).astype(BF16)
        out[:, :cut] = dot(h, down_own[0]).astype(BF16)
        out[:, cut:] = dot(h, down_rem[0]).astype(BF16)
        dx[:, :cut] = dot(dgu[...], gu_own[0]).astype(BF16)
        dx[:, cut:] = dot(dgu[...], gu_rem[0]).astype(BF16)
        totals[0][...] += dot(dgu[...], x_own, rows)
        totals[1][...] += dot(dgu[...], x_rem, rows)
        totals[2][...] += dot(h, d_own, rows)
        totals[3][...] += dot(h, d_rem, rows)

    @pl.when(meta[4, i] == 1)
    def _():
        for n, (total, to) in enumerate(zip(totals, results)):
            if later:
                to[0] = (total[...] + got[n][0].astype(F32)).astype(BF16)
            else:
                to[0] = total[...].astype(BF16)


def experts(plan, half, spot, x, d, weights, copies, got=(), filled=()):
    meta, source = plan["halves"][half]
    depth = x.shape[1]
    hidden, cut = weights[2].shape[1:]
    rest = depth - cut
    number = meta.shape[1]
    quarter = E // copies
    own_at = lambda i, meta, source, spot: (meta[0, i] ^ spot[1], 0, 0)
    rem_at = lambda i, meta, source, spot: (
        (((meta[0, i] ^ spot[1]) // quarter) ^ spot[0]) * quarter + meta[0, i] % quarter,
        0,
        0,
    )
    half_at = lambda i, meta, *_: (meta[0, i] - half * (E // 2), 0, 0)
    tile = pl.BlockSpec((TM, depth), lambda i, meta, *_: (meta[1, i], 0))
    shapes = [(2 * hidden, cut), (2 * hidden, rest), (hidden, cut), (hidden, rest)]
    anywhere = pl.BlockSpec(memory_space=pl.ANY)
    results = [pl.BlockSpec((1,) + s, half_at) for s in shapes]
    return pl.pallas_call(
        functools.partial(experts_body, (cut, number, hidden, half == 1)),
        grid_spec=pltpu.PrefetchScalarGridSpec(
            num_scalar_prefetch=3,
            grid=(number,),
            in_specs=[anywhere] * 2
            + [pl.BlockSpec((1,) + s, at) for s, at in zip(shapes, (own_at, rem_at) * 2)]
            + (results + [anywhere] * 2 if half else []),
            out_specs=[tile, tile] + results,
            scratch_shapes=[pltpu.VMEM((2, TM, depth), BF16)] * 2
            + [pltpu.VMEM((TM, 2 * hidden), BF16)]
            + [pltpu.VMEM(s, F32) for s in shapes]
            + [pltpu.SemaphoreType.DMA((2, 2))],
        ),
        out_shape=[jax.ShapeDtypeStruct((plan["number"] * TM, depth), BF16)] * 2
        + [jax.ShapeDtypeStruct((E // 2,) + s, BF16) for s in shapes],
        input_output_aliases={13: 0, 14: 1} if half else {},
        compiler_params=params(),
        cost_estimate=cost(9 * plan["number"] * TM * depth * hidden, 6 * E * depth * hidden + number * TM * depth * 4),
        name=("experts_first", "experts_second")[half],
    )(meta, source, spot, x, d, *weights, *got, *filled)


def from_ahead(values, shift):
    n = lax.axis_size("gy")
    return lax.ppermute(values, "gy", [(s, (s - shift) % n) for s in range(n)])


def across(values, bit):
    n = lax.axis_size("dp")
    return lax.ppermute(values, "dp", [(d, d ^ bit) for d in range(n)])


def bits():
    n, bit, out = lax.axis_size("dp"), 1, []
    while bit < n:
        out.append(bit)
        bit *= 2
    return out


def tie(values, *others):
    return lax.optimization_barrier((values, others))[0]


class Spread:
    def __init__(self, weights):
        self.weights = weights

    def cut(self):
        copies, me = lax.axis_size("dp"), lax.axis_index("dp")
        return [
            lax.dynamic_slice_in_dim(w, me * (w.shape[0] // copies), w.shape[0] // copies)
            for w, _ in self.weights
        ]

    def over_gy(self, pieces):
        parts = lax.axis_size("gy")
        out = []
        for piece, (_, axis) in zip(pieces, self.weights):
            got = [from_ahead(piece, k) for k in range(1, parts)]
            out.append({0: got[0] if len(got) == 1 else jnp.concatenate(got, axis=axis)})
        return out

    def over_dp(self, held, level):
        bit = list(reversed(bits()))[level]
        return [h | {key | bit: across(part, bit) for key, part in h.items()} for h in held]


def keyed(held):
    return jnp.concatenate([held[key] for key in range(len(held))], axis=0)


def whole(weight, axis, held):
    me = lax.axis_index("dp")
    stack = [held[key] for key in range(len(held))]
    for bit in bits():
        swap = (me & bit) != 0
        stack = [jnp.where(swap, stack[n ^ bit], stack[n]) for n in range(len(stack))]
    return jnp.concatenate([weight, jnp.concatenate(stack, axis=0)], axis=axis)


def to_rows(values):
    parts, me = lax.axis_size("gy"), lax.axis_index("gy")
    share = values.shape[0] // parts
    take = lambda k: lax.dynamic_slice_in_dim(values, ((me - k + parts) % parts) * share, share)
    return jnp.concatenate(
        [take(0)] + [from_ahead(take(k), k) for k in range(1, parts)], axis=1
    )


def to_columns(values, kind):
    parts, me = lax.axis_size("gy"), lax.axis_index("gy")
    width = values.shape[1] // parts
    blocks = []
    for k in range(parts):
        block = values[:, k * width : (k + 1) * width]
        blocks.append((from_ahead(block.astype(BF16), parts - k) if k else block).astype(kind))
    return jnp.concatenate(in_order([blocks[(parts - k) % parts] for k in range(parts)], me), axis=0)


def in_order(blocks, me):
    n = len(blocks)
    out = []
    for place in range(n):
        block = blocks[place]
        for k in range(n):
            block = jnp.where(me == (place - k) % n, blocks[k], block)
        out.append(block)
    return out


class Reduce:
    def __init__(self):
        self.side = lax.axis_index("dp") & 1

    def pick(self, values, side):
        half = values.shape[0] // 2
        return lax.dynamic_slice_in_dim(values, side * half, half)

    def near(self, grads):
        sums = []
        for grad in grads:
            sums.append([])
            for v in grad:
                got = across(self.pick(v, 1 - self.side), 1)
                sums[-1].append((self.pick(v, self.side).astype(F32) + got.astype(F32)).astype(BF16))
        return sums

    def over_gy(self, sums):
        parts = lax.axis_size("gy")
        out = []
        for own, *rest in sums:
            total = own.astype(F32)
            for k, piece in enumerate(rest, start=1):
                total = total + from_ahead(piece, parts - k).astype(F32)
            out.append(total.astype(BF16))
        return out

    def over_dp(self, sums):
        for bit in bits()[1:]:
            sums = [(t.astype(F32) + across(t, bit).astype(F32)).astype(BF16) for t in sums]
        return sums

    def finish(self, sums):
        out = []
        for total in sums:
            other = across(total, 1)
            first = jnp.where(self.side == 0, total, other).astype(F32)
            second = jnp.where(self.side == 0, other, total).astype(F32)
            out.append(jnp.concatenate([first, second], axis=0))
        return out


def split_blocks(values, parts, axis):
    width = values.shape[axis] // parts
    return [lax.slice_in_dim(values, k * width, (k + 1) * width, axis=axis) for k in range(parts)]


def gather_rows(values):
    return lax.all_gather(values, "gx", axis=0, tiled=True)


def sum_rows(values):
    return lax.psum_scatter(values, "gx", scatter_dimension=0, tiled=True)


def local(
    stream_in, lengths, routes, route_weights, norm_attn, w_qkv, qkv_bias, w_out, norm_ffn, w_gate, w_up,
    w_down, shared_gate, shared_up, shared_down, shared_router, cotangent
):
    parts, gy = lax.axis_size("gy"), lax.axis_index("gy")
    groups, gx = lax.axis_size("gx"), lax.axis_index("gx")
    dp = lax.axis_index("dp")
    held, width = stream_in.shape
    depth = width * parts
    size = held // parts
    rows = size * groups
    heads = qkv_bias.shape[0]
    count = lengths.shape[0]

    numbers = jnp.arange(count)
    ends = jnp.sum(jnp.where(numbers[:, None] <= numbers[None, :], lengths[:, None], 0), axis=0)
    ends = ends.astype(jnp.int32)
    row = jnp.arange(rows, dtype=jnp.int32)
    place = (row // size) * held + gy * size + row % size
    begin = jnp.zeros_like(place)
    for n in range(count):
        begin = jnp.where(place >= ends[n], ends[n], begin)
    mine = gx * held + gy * size + jnp.arange(size, dtype=jnp.int32)
    valid = (mine < ends[count - 1]).astype(F32)[:, None]
    half = HD // 2
    angles = (place - begin).astype(F32)[:, None] * (
        THETA ** (-jnp.arange(half, dtype=F32) * 2.0 / HD)
    )[None, :]
    cos, sin = jnp.cos(angles), jnp.sin(angles)
    cos = jnp.concatenate([cos, cos], axis=1)
    sin = jnp.concatenate([-sin, sin], axis=1)
    span = jnp.concatenate([ends, gy[None].astype(jnp.int32)])

    narrow = jnp.concatenate([norm_attn[None], norm_ffn[None], shared_router[None]])
    stream_rows, dy_rows = to_rows(stream_in), to_rows(cotangent)
    narrow = jnp.concatenate([narrow] + [from_ahead(narrow, k) for k in range(1, parts)], axis=1)
    gain_attn, gain_ffn, router = (narrow[n].astype(F32)[None, :] for n in range(3))
    flat_qkv = w_qkv.reshape(width, heads * 3 * HD)
    lead = Spread([(flat_qkv, 0), (w_out, 1)])
    gate_t, up_t = jnp.swapaxes(w_gate, 1, 2), jnp.swapaxes(w_up, 1, 2)
    early = Spread([(shared_gate, 0), (shared_up, 0), (shared_down, 1), (gate_t, 2)])
    late = [Spread([(up_t, 2)]), Spread([(w_down, 2)])]

    stream = stream_rows.astype(F32)
    inv_attn = lax.rsqrt(jnp.mean(stream * stream, axis=1, keepdims=True) + EPS)
    unit_attn = stream * inv_attn
    n1_part = (unit_attn * gain_attn).astype(BF16)
    lead_held = lead.over_gy(tie(lead.cut(), stream_rows))
    masked = dy_rows.astype(F32) * valid
    dy_part = masked.astype(BF16)
    early_held = early.over_gy(tie(early.cut(), dy_rows))
    n1 = gather_rows(n1_part)
    lead_held = lead.over_dp(lead_held, 0)
    lead_held = lead.over_dp(lead_held, 1)
    qkv_all = whole(flat_qkv, 0, lead_held[0])
    out_all = whole(w_out, 1, lead_held[1])
    n1, dy_part, qkv_all, out_all = lax.optimization_barrier((n1, dy_part, qkv_all, out_all))
    dy = gather_rows(dy_part)

    q, kv = project_qkv(n1, qkv_all, qkv_bias, cos, sin)
    kv, early_held = lax.optimization_barrier((kv, early_held))
    kv_rest = [from_ahead(kv, k) for k in range(1, parts)]
    kv_rest = kv_rest[0] if parts == 2 else jnp.concatenate(kv_rest, axis=0)
    shared_held, gate_held = early_held[:3], early_held[3:]
    gate_held = early.over_dp(gate_held, 0)
    kv_rest, gate_held = lax.optimization_barrier((kv_rest, gate_held))
    shared_held = early.over_dp(shared_held, 0)
    up_held = late[0].over_gy(tie(late[0].cut(), kv_rest))
    o, o_exact, level = attend(span, q, kv, kv_rest, size, parts, count)
    o, up_held, shared_held = lax.optimization_barrier((o, up_held, shared_held))
    attn_part = dot(o, out_all).astype(BF16)
    attn_part, dy = lax.optimization_barrier((attn_part, dy))
    attn = sum_rows(attn_part).astype(F32)
    down_held = late[1].over_gy(tie(late[1].cut(), o))
    shared_held = early.over_dp(shared_held, 1)
    gate_held = early.over_dp(gate_held, 1)
    up_held = late[0].over_dp(up_held, 0)

    block = 256 if rows % 256 == 0 else 128
    shape = (rows // block, block, depth)
    take = lambda v: lax.dynamic_index_in_dim(
        v.reshape(groups, parts, size, v.shape[1]), gy, 1, keepdims=False
    ).reshape(rows, v.shape[1])
    flip = (1 - (dp & 1)) * (E // 2)
    plan = plan_tiles(take(routes) ^ flip, take(route_weights), block)
    spot = jnp.stack([dp, flip]).astype(jnp.int32)
    d_slots = send_out(plan, dy.reshape(shape), True)
    sg_all = whole(shared_gate, 0, shared_held[0])
    su_all = whole(shared_up, 0, shared_held[1])
    sd_all = whole(shared_down, 1, shared_held[2])
    cols, both = ((1,), (1,)), ((0,), (0,))
    d_s_hidden = dot(dy, sd_all, cols)

    middle = stream + attn
    inv_ffn = lax.rsqrt(jnp.mean(middle * middle, axis=1, keepdims=True) + EPS)
    unit_ffn = middle * inv_ffn
    n2_part = (unit_ffn * gain_ffn).astype(BF16)
    n2_part, up_held, down_held, d_slots, d_s_hidden, plan["halves"] = lax.optimization_barrier(
        (n2_part, up_held, down_held, d_slots, d_s_hidden, plan["halves"])
    )
    n2 = gather_rows(n2_part)
    up_held = late[0].over_dp(up_held, 1)
    down_held = late[1].over_dp(down_held, 0)
    down_held = late[1].over_dp(down_held, 1)
    copies = lax.axis_size("dp")
    weights = [
        jnp.concatenate([gate_t, up_t], axis=1),
        jnp.concatenate(
            [jnp.concatenate([gate_held[0][key], up_held[0][key]], axis=1) for key in range(copies)], axis=0
        ),
        w_down,
        keyed(down_held[0]),
    ]

    n2, weights = lax.optimization_barrier((n2, weights))
    x_slots = send_out(plan, n2.reshape(shape), False)
    out_slots, dx_slots, *given = experts(plan, 0, spot, x_slots, d_slots, weights, copies)

    n2_s = tie(n2, given)
    got = [across(v, 1) for v in given]
    logit = jnp.sum(n2_s.astype(F32) * router, axis=1, keepdims=True)
    mixer = jax.nn.sigmoid(logit)
    sgate, sup = dot(n2_s, sg_all), dot(n2_s, su_all)
    s_logistic = jax.nn.sigmoid(sgate)
    s_act = sgate * s_logistic
    s_hidden = (mixer * s_act * sup).astype(BF16)
    d_sgate = (d_s_hidden * mixer * sup * s_logistic * (1.0 + sgate * (1.0 - s_logistic))).astype(BF16)
    d_sup = (d_s_hidden * mixer * s_act).astype(BF16)
    d_logit = jnp.sum(d_s_hidden * s_act * sup, axis=1, keepdims=True) * mixer * (1.0 - mixer)
    pieces = [
        [dot(a, d_sgate, both).astype(BF16) for a in split_blocks(n2_s, parts, 1)],
        [dot(a, d_sup, both).astype(BF16) for a in split_blocks(n2_s, parts, 1)],
        [dot(s_hidden, a, both).astype(BF16) for a in split_blocks(dy, parts, 1)],
    ]
    reduce = Reduce()
    shared_sums = reduce.near(pieces)
    dn2_shared = (
        dot(d_sgate, sg_all, cols) + dot(d_sup, su_all, cols) + d_logit * router
    ).astype(BF16)

    x_slots, shared_sums, dn2_shared, got = lax.optimization_barrier(
        (x_slots, shared_sums, dn2_shared, got)
    )
    out_slots, dx_slots, *sums = experts(
        plan, 1, spot, x_slots, d_slots, weights, copies, got, (out_slots, dx_slots)
    )
    shared_sums = reduce.over_gy(shared_sums)
    dx_slots, out_slots, shared_sums, sums = lax.optimization_barrier(
        (dx_slots, out_slots, shared_sums, sums)
    )
    down_sums = [[sums[2]] + split_blocks(sums[3], parts - 1, 2)]
    cuts = (0, E // 4, 3 * E // 8, E // 2)
    gu_sums = [
        [[sums[0][low:high]] + split_blocks(sums[1][low:high], parts - 1, 2)]
        for low, high in zip(cuts, cuts[1:])
    ]
    dn2 = bring_back(plan, dx_slots, block, False)
    dn2 = (dn2.reshape(rows, depth).astype(F32) + dn2_shared.astype(F32)).astype(BF16)
    d_n2 = sum_rows(dn2).astype(F32)
    down_sums = reduce.over_gy(down_sums)
    shared_sums = reduce.over_dp(shared_sums)
    routed = bring_back(plan, tie(out_slots, dn2), block, True)
    branch_part = (routed.reshape(rows, depth).astype(F32) + dot(s_hidden, sd_all)).astype(BF16)
    router_part = jnp.sum(d_logit * n2_s.astype(F32), axis=0)

    gain_ffn_part = jnp.sum(d_n2 * unit_ffn, axis=0)
    scaled = d_n2 * gain_ffn
    d_middle = masked + inv_ffn * (
        scaled - unit_ffn * jnp.mean(scaled * unit_ffn, axis=1, keepdims=True)
    )

    d_mid_part = d_middle.astype(BF16)
    d_mid_part, down_sums, branch_part, shared_sums, gu_sums = lax.optimization_barrier(
        (d_mid_part, down_sums, branch_part, shared_sums, gu_sums)
    )
    d_mid = gather_rows(d_mid_part)
    gu_sums[0] = reduce.over_gy(gu_sums[0])
    down_sums = reduce.over_dp(down_sums)
    grad_sgate, grad_sup, grad_sdown = reduce.finish(shared_sums)
    d_mid, gu_sums, down_sums, branch_part = lax.optimization_barrier(
        (d_mid, gu_sums, down_sums, branch_part)
    )
    branch = sum_rows(branch_part).astype(F32)
    d_o = dot(d_mid, out_all, cols).astype(BF16)
    gu_sums[0] = reduce.over_dp(gu_sums[0])
    gu_sums[1] = reduce.over_gy(gu_sums[1])
    dq, dkv_own, dkv_rest = attend_back(
        span, q, kv, kv_rest, d_o, o_exact, level, cos, sin, size, parts, count
    )
    dkv_rest, gu_sums[1:] = lax.optimization_barrier((dkv_rest, gu_sums[1:]))
    out_sums = reduce.near([[dot(o, b, both).astype(BF16) for b in split_blocks(d_mid, parts, 1)]])
    got = [
        from_ahead(piece, parts - k)
        for k, piece in enumerate(split_blocks(dkv_rest, parts - 1, 0), start=1)
    ]
    [grad_down] = reduce.finish(down_sums)
    got, out_sums, gu_sums = lax.optimization_barrier((got, out_sums, gu_sums))
    gu_sums[1] = reduce.over_dp(gu_sums[1])
    gu_sums[2] = reduce.over_gy(gu_sums[2])
    d_mixed, bias_part = mix_back(dq, dkv_own, got, cos, sin)
    d_n1_part = dot(d_mixed, qkv_all, cols).astype(BF16)
    d_n1 = sum_rows(d_n1_part).astype(F32)
    d_mixed = tie(d_mixed, d_n1_part)
    qkv_sums = reduce.near([[dot(a, d_mixed, both).astype(BF16) for a in split_blocks(n1, parts, 1)]])
    attn_sums = reduce.over_gy(qkv_sums + out_sums)
    gu_sums[2] = reduce.over_dp(gu_sums[2])
    grad_w_qkv, grad_w_out = reduce.finish(reduce.over_dp(attn_sums))
    grad_w_qkv = grad_w_qkv.reshape(width, heads, 3 * HD)
    result = middle + branch

    sums = jnp.stack([gain_ffn_part, router_part])
    sums = lax.dynamic_slice_in_dim(
        jnp.concatenate([sums, sums], axis=1), ((parts - gy) % parts) * width, depth, axis=1
    )
    flat_bias = bias_part.reshape(-1)
    biases = lax.dynamic_update_slice_in_dim(
        jnp.zeros((groups * flat_bias.shape[0],), F32), flat_bias, gx * flat_bias.shape[0], 0
    )
    squares = jnp.stack(
        [jnp.sum(valid * v * v) for v in (middle, result, attn, branch)] + [jnp.sum(valid) * depth]
    )
    sums = tie(jnp.concatenate([sums.reshape(-1), biases, squares]), d_n1_part)
    sums = lax.psum(sums, ("dp", "gx", "gy"))
    d_n1, sums = lax.optimization_barrier((d_n1, sums))
    hidden = gate_t.shape[1]
    gu = [gu_sum for [gu_sum] in gu_sums]
    gu_other = [across(v, 1) for v in gu]
    side = dp & 1
    grad_gate, grad_up = (
        jnp.swapaxes(
            jnp.concatenate(
                [jnp.where(side == 0, a[:, part], b[:, part]) for a, b in zip(gu, gu_other)]
                + [jnp.where(side == 0, b[:, part], a[:, part]) for a, b in zip(gu, gu_other)],
                axis=0,
            ).astype(F32),
            1,
            2,
        )
        for part in (slice(0, hidden), slice(hidden, 2 * hidden))
    )
    gain_attn_part = jnp.sum(d_n1 * unit_attn, axis=0)
    scaled = d_n1 * gain_attn
    grad_stream = d_middle + inv_attn * (
        scaled - unit_attn * jnp.mean(scaled * unit_attn, axis=1, keepdims=True)
    )

    def added(vectors):
        own, *rest = split_blocks(vectors, parts, 1)
        for k, piece in enumerate(rest, start=1):
            own = own + from_ahead(piece, parts - k)
        return jnp.sum(lax.all_gather(own, ("dp", "gx")), axis=0)

    [gain_sum] = added(gain_attn_part[None])
    vectors = lax.dynamic_slice_in_dim(sums[: 2 * depth].reshape(2, depth), gy * width, width, axis=1)
    bias_sum = lax.dynamic_slice_in_dim(sums[2 * depth : -5], gx * flat_bias.shape[0], flat_bias.shape[0])
    bias_sum = bias_sum.reshape(heads, 3 * HD)
    rms_stats = jnp.sqrt(sums[-5:-1] / sums[-1])
    return (
        to_columns(result, BF16),
        to_columns(grad_stream, F32),
        gain_sum,
        grad_w_qkv,
        bias_sum,
        grad_w_out,
        vectors[0],
        grad_gate,
        grad_up,
        grad_down,
        grad_sgate,
        grad_sup,
        grad_sdown,
        vectors[1],
        rms_stats,
    )


def solution(mesh):
    placed = (
        P(("dp", "gx"), "gy"),
        P("dp"),
        P("dp", None),
        P("dp", None),
        P("gy"),
        P("gy", "gx", None),
        P("gx", None),
        P("gx", "gy"),
        P("gy"),
        P(None, "gy", "gx"),
        P(None, "gy", "gx"),
        P(None, "gx", "gy"),
        P("gy", "gx"),
        P("gy", "gx"),
        P("gx", "gy"),
        P("gy"),
        P(("dp", "gx"), "gy"),
    )
    return jax.shard_map(
        local,
        mesh=mesh,
        in_specs=placed,
        out_specs=(
            P(("dp", "gx"), "gy"),
            P(("dp", "gx"), "gy"),
            P("gy"),
            P("gy", "gx", None),
            P("gx", None),
            P("gx", "gy"),
            P("gy"),
            P(None, "gy", "gx"),
            P(None, "gy", "gx"),
            P(None, "gx", "gy"),
            P("gy", "gx"),
            P("gy", "gx"),
            P("gx", "gy"),
            P("gy"),
            P(),
        ),
        check_vma=False,
    )
```

time: 5900 us -> 1860 us (0.32)
  waiting for transfers between devices: 3500 us -> 556 us
  local copies, waits for them, and re-layouts: 1050 us -> 89.6 us
  matrix products: 881 us -> 214 us
  Pallas kernels: 0 us -> 402 us
  starting transfers between devices: 2.33 us -> 105 us
  other arithmetic: 320 us -> 381 us
    reduce_scatter x9 -> x0, waiting for transfers between devices: 1270 us -> none  [the longest x3 378 us: sum_query(): return lax.psum_scatter(values, 'gy', scatter_dimension=0, tiled=True)]
    psum x1 -> x0, waiting for transfers between devices: 756 us -> none  [local(): lax.psum(grad_w_qkv.astype(jnp.bfloat16), 'dp').astype(jnp.float32)]
    dot_general x53 -> x20, matrix products: 881 us -> 214 us  [the longest x19 214 us: dot(): return lax.dot_general(a, b, (dims, ((), ())), preferred_element_type=F32)]
    gather x4 -> x0, local copies, waits for them, and re-layouts: 653 us -> none  [the longest x1 234 us: local(): picked_grad[slot_of].reshape(SLOTS, TOPK, width_part)]
    reduce_scatter x4, waiting for transfers between devices: 583 us -> 0.01 us  [sum_rows(): return lax.psum_scatter(values, 'gx', scatter_dimension=0, tiled=True)]
    ppermute x0 -> x81, waiting for transfers between devices: none -> 515 us  [the longest x56 400 us: across(): return lax.ppermute(values, 'dp', [(d, d ^ bit) for d in range(n)])]
    all_gather x10 -> x0, waiting for transfers between devices: 457 us -> none  [the longest x1 142 us: local(): lax.all_gather(gate_grad, 'gy', axis=0, tiled=True)]
    pallas_call x0 -> x10, Pallas kernels: none -> 402 us  [the longest x2 206 us: experts(): pl.pallas_call(functools.partial(experts_body, (cut, number, hidden, half...]
  transfers between devices with their start and end apart: 28 -> 89, of which waited for: 21 -> 23; matrix products, arithmetic and copies ran while one was open for 30% -> 32% of each run, Pallas kernels for 0% -> 14%
where the time goes in v1:
time: 1860 us; the launch traced here: 1840 us
  waiting for transfers between devices  556 us (30%)
  Pallas kernels  402 us (22%)
  other arithmetic  381 us (20%)
  matrix products  214 us (12%)
  starting transfers between devices  105 us (6%)
  local copies, waits for them, and re-layouts  89.6 us (5%)
  blocking collectives  69 us (4%)
    ppermute x56, waiting for transfers between devices, across(): return lax.ppermute(values, 'dp', [(d, d ^ bit) for d in range(n)])  400 us
    dot_general x19, matrix products, dot(): return lax.dot_general(a, b, (dims, ((), ())), preferred_element_type=F32)  214 us
    pallas_call x2, Pallas kernels, experts(): pl.pallas_call(functools.partial(experts_body, (cut, number, hidden, half...  206 us
    ppermute x25, waiting for transfers between devices, from_ahead(): return lax.ppermute(values, 'gy', [(s, (s - shift) % n) for s in range(n)])  115 us
    ppermute x56, starting transfers between devices, across(): return lax.ppermute(values, 'dp', [(d, d ^ bit) for d in range(n)])  74.7 us
    unnamed x28, other arithmetic  51.1 us
    pallas_call x1, Pallas kernels, attend_back(): pl.pallas_call(functools.partial(attend_back_body, (size, blocks, parts,...  47.3 us
    convert_element_type x9, other arithmetic, over_dp(): (t.astype(F32) + across(t, bit).astype(F32)).astype(BF16)  46.5 us
  transfers between devices with their start and end apart: 89, of which 23 were waited for; matrix products, arithmetic and copies ran while one was open for 32% of the time, Pallas kernels for 14%

profile of v1, /device:TPU:0, one launch (start us, length us, event | category | flops | bytes accessed | tf_op | source)
XLA Modules:
  0.0 1835.4 jit_solution(10663038596492399339)
XLA Ops:
  12.0 17.5 collective-permute-done.1
  108.5 40.7 %all-gather.7.cloned.1.call-done.n1 = bf16[1536,2048]{1,0:T(8,128)(2,1)} async-done(((bf16[384,2048]{1,0:T(8,128)(2,1)}), bf16[1536,2048]{1,0:T(8,128)(2,1)}) %all-gather.7.cloned.1.call-update) | async-done | bytes 6291472 | tf_op jit(solution)/shard_map/all_gather | solution.py:730
  159.5 19.3 %project_qkv.1 = (bf16[1536,512]{1,0:T(8,128)(2,1)}, bf16[1536,1024]{1,0:T(8,128)(2,1)}) custom-call(bf16[1536,2048]{1,0:T(8,128)(2,1)} %all-gather.7.cloned.1.call-done.n1, bf16[2048,1536]{1,0:T(8,128)(2,1)} %select_dynamic-update-slice_fusion.12.w, bf16[4,1,384]{2,1,0:T(2,128)(2,1)} %copy.113.bias, f32[1536,128]{1,0:T(8,128)} %get-tuple-element.370.cos.refs_1_, ...), custom_call_target="tpu_custom_call" | custom-call | flops 9663676416 | bytes 12582912 | tf_op jit(solution)/shard_map/project_qkv/pallas_call | solution.py:59
  184.2 14.7 collective-permute-done.13
  201.8 62.2 %collective-permute-done.16 = bf16[4,352,1024]{2,1,0:T(8,128)(2,1)} collective-permute-done((bf16[4,352,1024]{2,1,0:T(8,128)(2,1)}, bf16[4,352,1024]{2,1,0:T(8,128)(2,1)}, u32[]{:S(2)}, u32[]{:S(2)}) %collective-permute-start.16) | collective-permute-done | bytes 2883616 | tf_op jit(solution)/shard_map/ppermute | solution.py:600
  274.0 43.8 %attend.1 = (bf16[1536,512]{1,0:T(8,128)(2,1)}, f32[1536,512]{1,0:T(8,128)}, f32[1536,512]{1,0:T(8,128)}) custom-call(s32[3]{0:T(128)} %pad_add_fusion.meta, bf16[1536,512]{1,0:T(8,128)(2,1)} %get-tuple-element.144.q, bf16[1536,1024]{1,0:T(8,128)(2,1)} %get-tuple-element.150.kv_own, bf16[1536,1024]{1,0:T(8,128)(2,1)} %collective-permute-done.15.kv_rem), custom_call_target="tpu_custom_call" | custom-call | flops 14495514624 | bytes 23592960 | tf_op jit(solution)/shard_map/attend/pallas_call | solution.py:162
  317.9 13.6 collective-permute-done.17
  365.0 24.4 %pad_maximum_fusion.gu_own = bf16[16,704,1024]{2,1,0:T(8,128)(2,1)} fusion(bf16[16,352,1024]{2,1,0:T(8,128)(2,1)} %bitcast.142, bf16[16,352,1024]{2,1,0:T(8,128)(2,1)} %bitcast.143), kind=kLoop, calls=%fused_computation | loop fusion | flops 46137344 | bytes 46137344 | tf_op jit(solution)/shard_map/concatenate | solution.py:843
  395.0 40.3 %fusion.82 = f32[1536,1408]{1,0:T(8,128)} fusion(bf16[1536,2048]{1,0:T(8,128)(2,1)} %all-gather.9.cloned.1.call-done, bf16[352,1024]{1,0:T(8,128)(2,1)S(1)} %get-tuple-element.334, bf16[352,1024]{1,0:T(8,128)(2,1)S(1)} %get-tuple-element.333, bf16[352,1024]{1,0:T(8,128)(2,1)S(1)} %get-tuple-element.332, bf16[352,1024]{1,0:T(8,128)(2,1)S(1)} %get-tuple-element.331, ...), kind=kOutput, calls=%fused_computation.348 | convolution fusion | flops 8887205888 | bytes 20709376 | tf_op jit(solution)/shard_map/dot_general | solution.py:27
  435.4 17.7 send_out.2
  477.7 53.0 %collective-permute-done.30 = bf16[4,352,1024]{2,1,0:T(8,128)(2,1)} collective-permute-done((bf16[4,352,1024]{2,1,0:T(8,128)(2,1)}, bf16[4,352,1024]{2,1,0:T(8,128)(2,1)}, u32[]{:S(2)}, u32[]{:S(2)}) %collective-permute-start.30) | collective-permute-done | bytes 2883616 | tf_op jit(solution)/shard_map/ppermute | solution.py:600
  530.7 31.9 %maximum_maximum_fusion.gu_rem = bf16[16,704,1024]{2,1,0:T(8,128)(2,1)} fusion(bf16[4,352,1024]{2,1,0:T(8,128)(2,1)} %collective-permute-done.28, bf16[4,352,1024]{2,1,0:T(8,128)(2,1)} %collective-permute-done.27, bf16[4,352,1024]{2,1,0:T(8,128)(2,1)} %collective-permute-done.21, bf16[4,352,1024]{2,1,0:T(8,128)(2,1)} %collective-permute-done.16, ...), kind=kLoop, calls=%fused_computation.1 | loop fusion | flops 184549376 | bytes 46137344 | tf_op jit(solution)/shard_map/concatenate | solution.py:844
  570.9 15.1 send_out.3
  586.1 103.8 %experts_first.1 = (bf16[11520,2048]{1,0:T(8,128)(2,1)}, bf16[11520,2048]{1,0:T(8,128)(2,1)}, bf16[8,704,1024]{2,1,0:T(8,128)(2,1)}, bf16[8,704,1024]{2,1,0:T(8,...) custom-call(s32[6,34]{1,0:T(8,128)} %stack.56.meta, s32[34,16]{1,0:T(8,128)} %copy.122.source, ...), custom_call_target="tpu_custom_call" | custom-call | flops 74742497280 | bytes 140509184 | tf_op jit(solution)/shard_map/experts_first/pallas_call | solution.py:570
  689.9 15.5 fusion.90
  706.7 19.8 %multiply_reduce_fusion = (f32[1536]{0:T(1024)S(1)}, bf16[1536,1408]{1,0:T(8,128)(2,1)}, bf16[1536,1408]{1,0:T(8,128)(2,1)}, bf16[1536,1408]{1,0:T(8,128)(2,1)}) fusion(f32[1536,1408]{1,0:T(8,128)} %fusion.82, f32[1536,1408]{1,0:T(8,128)} %fusion.90, f32[1536]{0:T(1024)S(1)} %add_divide_fusion.1, bf16[1536,2048]{1,0:T(8,128)(2,1)S(1)} %bitcast.127, ...), kind=kOutput, calls=%fused_computation.19 | convolution fusion | flops 8901621760 | bytes 42348544 | tf_op jit(solution)/shard_map/dot_general | solution.py:27
  772.9 16.9 add_convert_fusion
  825.9 101.8 %experts_second.1 = (bf16[11520,2048]{1,0:T(8,128)(2,1)}, bf16[11520,2048]{1,0:T(8,128)(2,1)}, bf16[8,704,1024]{2,1,0:T(8,128)(2,1)}, bf16[8,704,1024]{2,1,0:T(8...) custom-call(s32[6,34]{1,0:T(8,128)} %stack.58.meta, ...), custom_call_target="tpu_custom_call", output_to_operand_aliasing={{0}: (13, {}), {1}: (14, {})} | custom-call | flops 74742497280 | bytes 140509184 | tf_op jit(solution)/shard_map/experts_second/pallas_call | solution.py:570
  934.5 21.4 %bring_back.2 = bf16[6,256,2048]{2,1,0:T(8,128)(2,1)} custom-call(s32[6,79]{1,0:T(8,128)} %select_reduce_fusion.3.get, s32[6,256,4]{2,1,0:T(8,128)} %bitcast.147, bf16[11520,2048]{1,0:T(8,128)(2,1)} %get-tuple-element.212.refs_0_), custom_call_target="tpu_custom_call" | custom-call | flops 7952400384 | bytes 62128128 | tf_op jit(solution)/shard_map/bring_back/pallas_call | solution.py:464
  970.6 23.6 %bring_back.3 = bf16[6,256,2048]{2,1,0:T(8,128)(2,1)} custom-call(s32[6,79]{1,0:T(8,128)} %select_reduce_fusion.3.get, s32[6,256,4]{2,1,0:T(8,128)} %bitcast.148, f32[6,256,4]{2,1,0:T(8,128)} %bitcast.152, bf16[11520,2048]{1,0:T(8,128)(2,1)} %get-tuple-element.217.refs_1_), custom_call_target="tpu_custom_call" | custom-call | flops 7952400384 | bytes 62128128 | tf_op jit(solution)/shard_map/bring_back/pallas_call | solution.py:464
  994.1 17.5 fusion.2
  1036.4 20.2 %collective-permute-done.50 = bf16[512,1408]{1,0:T(8,128)(2,1)} collective-permute-done((bf16[512,1408]{1,0:T(8,128)(2,1)}, bf16[512,1408]{1,0:T(8,128)(2,1)}, u32[]{:S(2)}, u32[]{:S(2)}) %collective-permute-start.50) | collective-permute-done | bytes 1441824 | tf_op jit(solution)/shard_map/ppermute | solution.py:600
  1059.5 26.5 %collective-permute-done.49 = bf16[8,352,1024]{2,1,0:T(8,128)(2,1)} collective-permute-done((bf16[8,352,1024]{2,1,0:T(8,128)(2,1)}, bf16[8,352,1024]{2,1,0:T(8,128)(2,1)}, u32[]{:S(2)}, u32[]{:S(2)}) %collective-permute-start.49) | collective-permute-done | bytes 5767200 | tf_op jit(solution)/shard_map/ppermute | solution.py:595
  1125.7 93.4 %collective-permute-done.54 = bf16[8,352,1024]{2,1,0:T(8,128)(2,1)} collective-permute-done((bf16[8,352,1024]{2,1,0:T(8,128)(2,1)}, bf16[8,352,1024]{2,1,0:T(8,128)(2,1)}, u32[]{:S(2)}, u32[]{:S(2)}) %collective-permute-start.54) | collective-permute-done | bytes 5767200 | tf_op jit(solution)/shard_map/ppermute | solution.py:600
  1254.5 47.3 %attend_back.1 = (bf16[1536,512]{1,0:T(8,128)(2,1)}, f32[1536,1024]{1,0:T(8,128)}, bf16[1536,1024]{1,0:T(8,128)(2,1)}) custom-call(s32[3]{0:T(128)} %pad_add_fusion.meta, bf16[1536,512]{1,0:T(8,128)(2,1)} %get-tuple-element.144.q, bf16[1536,1024]{1,0:T(8,128)(2,1)} %get-tuple-element.150.kv_own, bf16[1536,1024]{1,0:T(8,128)(2,1)} %collective-permute-done.15.kv_rem, ...), custom_call_target="tpu_custom_call" | custom-call | flops 24159191040 | bytes 31457280 | tf_op jit(solution)/shard_map/attend_back/pallas_call | solution.py:245
  1333.3 32.1 %collective-permute-done.60 = bf16[4,704,1024]{2,1,0:T(8,128)(2,1)} collective-permute-done((bf16[4,704,1024]{2,1,0:T(8,128)(2,1)}, bf16[4,704,1024]{2,1,0:T(8,128)(2,1)}, u32[]{:S(2)}, u32[]{:S(2)}) %collective-permute-start.60) | collective-permute-done | bytes 5767200 | tf_op jit(solution)/shard_map/ppermute | solution.py:600
  1385.9 15.6 convolution_convert_fusion
  1435.4 13.9 collective-permute-done.68
  1462.2 57.9 %collective-permute-done.69 = bf16[256,1024]{1,0:T(8,128)(2,1)S(1)} collective-permute-done((bf16[256,1024]{1,0:T(8,128)(2,1)S(1)}, bf16[256,1024]{1,0:T(8,128)(2,1)S(1)}, u32[]{:S(2)}, u32[]{:S(2)}) %collective-permute-start.69) | collective-permute-done | bytes 524320 | tf_op jit(solution)/shard_map/ppermute | solution.py:600
  1579.7 63.6 %collective-permute-done.66 = bf16[512,1536]{1,0:T(8,128)(2,1)} collective-permute-done((bf16[512,1536]{1,0:T(8,128)(2,1)}, bf16[512,1536]{1,0:T(8,128)(2,1)}, u32[]{:S(2)}, u32[]{:S(2)}) %collective-permute-start.66) | collective-permute-done | bytes 1572896 | tf_op jit(solution)/shard_map/ppermute | solution.py:600
  1687.8 37.3 %psum.7 = f32[10245]{0:T(1024)S(1)} all-reduce(f32[10245]{0:T(1024)S(1)} %concatenate.138), channel_id=1, replica_groups=mesh['dp'=4,'gx'=4,'gy'=2] {'dp','gx','gy'}, use_global_device_ids=true, to_apply=%region_43.44 | all-reduce | flops 10245 | bytes 81960 | tf_op jit(solution)/shard_map/psum | solution.py:959
  1791.9 31.7 %all-gather.1 = f32[16,1,1024]{2,1,0:T(1,128)S(1)} all-gather(f32[1,1,1024]{2,1,0:T(1,128)S(1)} %fusion.74), channel_id=2, replica_groups=mesh['dp'=4,'gx'=4,'gy'=2] {'dp','gx'}, dimensions={0}, use_global_device_ids=true | all-gather | bytes 69632 | tf_op jit(solution)/shard_map/all_gather | solution.py:987
  (600 shorter events, 663.2 us)
Async XLA Ops:
  7.2 142.0 %all-gather.7.cloned.1.call-start = ((), (), s32[]{:S(2)}) async-start(), calls=%async_computation.4 | async-start | bytes 7864320 | tf_op jit(solution)/shard_map/all_gather | solution.py:730
  32.2 307.5 %all-gather.9.cloned.1.call-start = ((), (), s32[]{:S(2)}) async-start(), calls=%async_computation.5 | async-start | bytes 7864320 | tf_op jit(solution)/shard_map/all_gather | solution.py:730
  63.9 135.0 %collective-permute-start.14 = (bf16[4,352,1024]{2,1,0:T(8,128)(2,1)}, bf16[4,352,1024]{2,1,0:T(8,128)(2,1)}, u32[]{:S(2)}, u32[]{:S(2)}) collective-permute-start(bf16[4,352,1024]{2,1,0:T(8,128)(2,1)} %get-tuple-element.149), channel_id=1, source_target_pairs={{0,1},{1,0},{2,3},{3,2},{4,5},{5,4},{6,7},{7,6},{8,9},{9,8},{10,11... | collective-permute-start | bytes 8650760 | tf_op jit(solution)/shard_map/ppermute | solution.py:595
  149.2 303.9 %reduce-scatter.5.cloned.1.call-start = ((), (), s32[]{:S(2)}) async-start(), calls=%async_computation.6 | async-start | bytes 7864320 | tf_op jit(solution)/shard_map/reduce_scatter | solution.py:734
  339.7 231.3 %all-gather.11.cloned.1.call-start = ((), (), s32[]{:S(2)}) async-start(), calls=%async_computation.7 | async-start | bytes 7864320 | tf_op jit(solution)/shard_map/all_gather | solution.py:730
  389.4 88.1 %collective-permute-start.25 = (bf16[4,352,1024]{2,1,0:T(8,128)(2,1)}, bf16[4,352,1024]{2,1,0:T(8,128)(2,1)}, u32[]{:S(2)}, u32[]{:S(2)}) collective-permute-start(bf16[4,352,1024]{2,1,0:T(8,128)(2,1)} %collective-permute-done.14), channel_id=1, source_target_pairs={{0,8},{8,0},{16,24},{24,16},{1,9},{9,1},{17,25},{25,17},{2,10},{10... | collective-permute-start | bytes 8650760 | tf_op jit(solution)/shard_map/ppermute | solution.py:600
  457.7 636.6 %reduce-scatter.7.cloned.1.call-start = ((), (), s32[]{:S(2)}) async-start(), calls=%async_computation.8 | async-start | bytes 7864320 | tf_op jit(solution)/shard_map/reduce_scatter | solution.py:734
  477.5 85.1 %collective-permute-start.29 = (bf16[4,352,1024]{2,1,0:T(8,128)(2,1)}, bf16[4,352,1024]{2,1,0:T(8,128)(2,1)S(1)}, u32[]{:S(2)}, u32[]{:S(2)}) collective-permute-start(bf16[4,352,1024]{2,1,0:T(8,128)(2,1)} %collective-permute-done.22), channel_id=1, source_target_pairs={{0,8},{8,0},{16,24},{24,16},{1,9},{9,1},{17,25},{25,17},{2,10},{10... | collective-permute-start | bytes 8650760 | tf_op jit(solution)/shard_map/ppermute | solution.py:600
  742.3 80.8 %collective-permute-start.42 = (bf16[8,704,1024]{2,1,0:T(8,128)(2,1)}, bf16[8,704,1024]{2,1,0:T(8,128)(2,1)}, u32[]{:S(2)}, u32[]{:S(2)}) collective-permute-start(bf16[8,704,1024]{2,1,0:T(8,128)(2,1)} %get-tuple-element.183), channel_id=1, source_target_pairs={{0,8},{8,0},{16,24},{24,16},{1,9},{9,1},{17,25},{25,17},{2,10},{10... | collective-permute-start | bytes 34603016 | tf_op jit(solution)/shard_map/ppermute | solution.py:600
  743.0 80.1 %collective-permute-start.43 = (bf16[8,704,1024]{2,1,0:T(8,128)(2,1)}, bf16[8,704,1024]{2,1,0:T(8,128)(2,1)}, u32[]{:S(2)}, u32[]{:S(2)}) collective-permute-start(bf16[8,704,1024]{2,1,0:T(8,128)(2,1)} %get-tuple-element.184), channel_id=1, source_target_pairs={{0,8},{8,0},{16,24},{24,16},{1,9},{9,1},{17,25},{25,17},{2,10},{10... | collective-permute-start | bytes 34603016 | tf_op jit(solution)/shard_map/ppermute | solution.py:600
  823.1 104.7 %collective-permute-start.48 = (bf16[704,1024]{1,0:T(8,128)(2,1)S(1)}, bf16[704,1024]{1,0:T(8,128)(2,1)}, u32[]{:S(2)}, u32[]{:S(2)}) collective-permute-start(bf16[704,1024]{1,0:T(8,128)(2,1)S(1)} %add_convert_fusion.19), channel_id=1, source_target_pairs={{0,1},{1,0},{2,3},{3,2},{4,5},{5,4},{6,7},{7,6},{8,9},{9,8},{10,11... | collective-permute-start | bytes 4325384 | tf_op jit(solution)/shard_map/ppermute | solution.py:595
  823.9 106.0 %collective-permute-start.47 = (bf16[512,1408]{1,0:T(8,128)(2,1)}, bf16[512,1408]{1,0:T(8,128)(2,1)}, u32[]{:S(2)}, u32[]{:S(2)}) collective-permute-start(bf16[512,1408]{1,0:T(8,128)(2,1)} %add_convert_fusion.21), channel_id=1, source_target_pairs={{0,1},{1,0},{2,3},{3,2},{4,5},{5,4},{6,7},{7,6},{8,9},{9,8},{10,11... | collective-permute-start | bytes 4325384 | tf_op jit(solution)/shard_map/ppermute | solution.py:595
  825.2 106.5 %collective-permute-start.46 = (bf16[512,1408]{1,0:T(8,128)(2,1)}, bf16[512,1408]{1,0:T(8,128)(2,1)}, u32[]{:S(2)}, u32[]{:S(2)}) collective-permute-start(bf16[512,1408]{1,0:T(8,128)(2,1)} %add_convert_fusion.23), channel_id=1, source_target_pairs={{0,1},{1,0},{2,3},{3,2},{4,5},{5,4},{6,7},{7,6},{8,9},{9,8},{10,11... | collective-permute-start | bytes 4325384 | tf_op jit(solution)/shard_map/ppermute | solution.py:595
  967.0 270.4 %all-gather.13.cloned.1.call-start = ((), (), s32[]{:S(2)}) async-start(), calls=%async_computation.9 | async-start | bytes 7864320 | tf_op jit(solution)/shard_map/all_gather | solution.py:730
  969.1 87.5 %collective-permute-start.50 = (bf16[512,1408]{1,0:T(8,128)(2,1)}, bf16[512,1408]{1,0:T(8,128)(2,1)}, u32[]{:S(2)}, u32[]{:S(2)}) collective-permute-start(bf16[512,1408]{1,0:T(8,128)(2,1)} %add_convert_fusion.18), channel_id=1, source_target_pairs={{0,16},{8,24},{16,0},{24,8},{1,17},{9,25},{17,1},{25,9},{2,18},{10... | collective-permute-start | bytes 4325384 | tf_op jit(solution)/shard_map/ppermute | solution.py:600
  969.2 116.8 %collective-permute-start.49 = (bf16[8,352,1024]{2,1,0:T(8,128)(2,1)}, bf16[8,352,1024]{2,1,0:T(8,128)(2,1)}, u32[]{:S(2)}, u32[]{:S(2)}) collective-permute-start(bf16[8,352,1024]{2,1,0:T(8,128)(2,1)} %get-tuple-element.215), channel_id=1, source_target_pairs={{0,1},{1,0},{2,3},{3,2},{4,5},{5,4},{6,7},{7,6},{8,9},{9,8},{10,11... | collective-permute-start | bytes 17301512 | tf_op jit(solution)/shard_map/ppermute | solution.py:595
  1100.9 564.2 %reduce-scatter.9.cloned.1.call-start = ((), (), s32[]{:S(2)}) async-start(), calls=%async_computation.10 | async-start | bytes 7864320 | tf_op jit(solution)/shard_map/reduce_scatter | solution.py:734
  1101.1 118.1 %collective-permute-start.54 = (bf16[8,352,1024]{2,1,0:T(8,128)(2,1)}, bf16[8,352,1024]{2,1,0:T(8,128)(2,1)}, u32[]{:S(2)}, u32[]{:S(2)}) collective-permute-start(bf16[8,352,1024]{2,1,0:T(8,128)(2,1)} %add_convert_fusion.4), channel_id=1, source_target_pairs={{0,16},{8,24},{16,0},{24,8},{1,17},{9,25},{17,1},{25,9},{2,18},{10... | collective-permute-start | bytes 17301512 | tf_op jit(solution)/shard_map/ppermute | solution.py:600
  1103.3 126.0 %collective-permute-start.53 = (bf16[4,704,1024]{2,1,0:T(8,128)(2,1)}, bf16[4,704,1024]{2,1,0:T(8,128)(2,1)}, u32[]{:S(2)}, u32[]{:S(2)}) collective-permute-start(bf16[4,704,1024]{2,1,0:T(8,128)(2,1)} %slice.168), channel_id=1, source_target_pairs={{0,1},{1,0},{2,3},{3,2},{4,5},{5,4},{6,7},{7,6},{8,9},{9,8},{10,11... | collective-permute-start | bytes 17301512 | tf_op jit(solution)/shard_map/ppermute | solution.py:595
  1121.8 115.7 %collective-permute-start.80 = (bf16[704,1024]{1,0:T(8,128)(2,1)}, bf16[704,1024]{1,0:T(8,128)(2,1)}, u32[]{:S(2)}, u32[]{:S(2)}) collective-permute-start(bf16[704,1024]{1,0:T(8,128)(2,1)} %add_convert_fusion.13), channel_id=1, source_target_pairs={{0,8},{8,0},{16,24},{24,16},{1,9},{9,1},{17,25},{25,17},{2,10},{10... | collective-permute-start | bytes 4325384 | tf_op jit(solution)/shard_map/ppermute | solution.py:600
  1121.9 121.1 %collective-permute-start.78 = (bf16[512,1408]{1,0:T(8,128)(2,1)}, bf16[512,1408]{1,0:T(8,128)(2,1)}, u32[]{:S(2)}, u32[]{:S(2)}) collective-permute-start(bf16[512,1408]{1,0:T(8,128)(2,1)} %add_convert_fusion.15), channel_id=1, source_target_pairs={{0,8},{8,0},{16,24},{24,16},{1,9},{9,1},{17,25},{25,17},{2,10},{10... | collective-permute-start | bytes 4325384 | tf_op jit(solution)/shard_map/ppermute | solution.py:600
  1237.4 527.7 %reduce-scatter.11.cloned.1.call-start = ((), (), s32[]{:S(2)}) async-start(), calls=%async_computation.11 | async-start | bytes 7864320 | tf_op jit(solution)/shard_map/reduce_scatter | solution.py:734
  1246.7 118.7 %collective-permute-start.60 = (bf16[4,704,1024]{2,1,0:T(8,128)(2,1)}, bf16[4,704,1024]{2,1,0:T(8,128)(2,1)}, u32[]{:S(2)}, u32[]{:S(2)}) collective-permute-start(bf16[4,704,1024]{2,1,0:T(8,128)(2,1)} %add_convert_fusion.3), channel_id=1, source_target_pairs={{0,16},{8,24},{16,0},{24,8},{1,17},{9,25},{17,1},{25,9},{2,18},{10... | collective-permute-start | bytes 17301512 | tf_op jit(solution)/shard_map/ppermute | solution.py:600
  1330.9 125.0 %collective-permute-start.77 = (bf16[8,352,1024]{2,1,0:T(8,128)(2,1)}, bf16[8,352,1024]{2,1,0:T(8,128)(2,1)}, u32[]{:S(2)}, u32[]{:S(2)}) collective-permute-start(bf16[8,352,1024]{2,1,0:T(8,128)(2,1)} %add_convert_fusion.2), channel_id=1, source_target_pairs={{0,8},{8,0},{16,24},{24,16},{1,9},{9,1},{17,25},{25,17},{2,10},{10... | collective-permute-start | bytes 17301512 | tf_op jit(solution)/shard_map/ppermute | solution.py:600
  1375.5 157.4 %collective-permute-start.74 = (bf16[2,704,1024]{2,1,0:T(8,128)(2,1)}, bf16[2,704,1024]{2,1,0:T(8,128)(2,1)}, u32[]{:S(2)}, u32[]{:S(2)}) collective-permute-start(bf16[2,704,1024]{2,1,0:T(8,128)(2,1)} %get-tuple-element.260), channel_id=1, source_target_pairs={{0,1},{1,0},{2,3},{3,2},{4,5},{5,4},{6,7},{7,6},{8,9},{9,8},{10,11... | collective-permute-start | bytes 8650760 | tf_op jit(solution)/shard_map/ppermute | solution.py:595
  1432.6 220.5 %collective-permute-start.71 = (bf16[4,704,1024]{2,1,0:T(8,128)(2,1)}, bf16[4,704,1024]{2,1,0:T(8,128)(2,1)}, u32[]{:S(2)}, u32[]{:S(2)}) collective-permute-start(bf16[4,704,1024]{2,1,0:T(8,128)(2,1)} %add_convert_fusion.1), channel_id=1, source_target_pairs={{0,8},{8,0},{16,24},{24,16},{1,9},{9,1},{17,25},{25,17},{2,10},{10... | collective-permute-start | bytes 17301512 | tf_op jit(solution)/shard_map/ppermute | solution.py:600
  1449.4 107.8 %collective-permute-start.72 = (bf16[2,704,1024]{2,1,0:T(8,128)(2,1)}, bf16[2,704,1024]{2,1,0:T(8,128)(2,1)}, u32[]{:S(2)}, u32[]{:S(2)}) collective-permute-start(bf16[2,704,1024]{2,1,0:T(8,128)(2,1)} %add_convert_fusion.8), channel_id=1, source_target_pairs={{0,16},{8,24},{16,0},{24,8},{1,17},{9,25},{17,1},{25,9},{2,18},{10... | collective-permute-start | bytes 8650760 | tf_op jit(solution)/shard_map/ppermute | solution.py:600
  1455.8 89.0 %collective-permute-start.63 = (bf16[512,1536]{1,0:T(8,128)(2,1)}, bf16[512,1536]{1,0:T(8,128)(2,1)}, u32[]{:S(2)}, u32[]{:S(2)}) collective-permute-start(bf16[512,1536]{1,0:T(8,128)(2,1)} %constant_dynamic-slice_fusion.1), channel_id=1, source_target_pairs={{0,8},{8,0},{16,24},{24,16},{1,9},{9,1},{17,25},{25,17},{2,10},{10... | collective-permute-start | bytes 4718600 | tf_op jit(solution)/shard_map/ppermute | solution.py:600
  1544.9 102.0 %collective-permute-start.75 = (bf16[2,704,1024]{2,1,0:T(8,128)(2,1)}, bf16[2,704,1024]{2,1,0:T(8,128)(2,1)}, u32[]{:S(2)}, u32[]{:S(2)}) collective-permute-start(bf16[2,704,1024]{2,1,0:T(8,128)(2,1)} %add_convert_fusion.6), channel_id=1, source_target_pairs={{0,16},{8,24},{16,0},{24,8},{1,17},{9,25},{17,1},{25,9},{2,18},{10... | collective-permute-start | bytes 8650760 | tf_op jit(solution)/shard_map/ppermute | solution.py:600
  1556.9 86.4 %collective-permute-start.66 = (bf16[512,1536]{1,0:T(8,128)(2,1)}, bf16[512,1536]{1,0:T(8,128)(2,1)}, u32[]{:S(2)}, u32[]{:S(2)}) collective-permute-start(bf16[512,1536]{1,0:T(8,128)(2,1)} %add_convert_fusion.10), channel_id=1, source_target_pairs={{0,16},{8,24},{16,0},{24,8},{1,17},{9,25},{17,1},{25,9},{2,18},{10... | collective-permute-start | bytes 4718600 | tf_op jit(solution)/shard_map/ppermute | solution.py:600
  1563.0 96.3 %collective-permute-start.73 = (bf16[2,704,1024]{2,1,0:T(8,128)(2,1)}, bf16[2,704,1024]{2,1,0:T(8,128)(2,1)}, u32[]{:S(2)}, u32[]{:S(2)}) collective-permute-start(bf16[2,704,1024]{2,1,0:T(8,128)(2,1)} %add_convert_fusion.7), channel_id=1, source_target_pairs={{0,8},{8,0},{16,24},{24,16},{1,9},{9,1},{17,25},{25,17},{2,10},{10... | collective-permute-start | bytes 8650760 | tf_op jit(solution)/shard_map/ppermute | solution.py:600
  1652.7 75.1 %collective-permute-start.76 = (bf16[2,704,1024]{2,1,0:T(8,128)(2,1)}, bf16[2,704,1024]{2,1,0:T(8,128)(2,1)}, u32[]{:S(2)}, u32[]{:S(2)}) collective-permute-start(bf16[2,704,1024]{2,1,0:T(8,128)(2,1)} %add_convert_fusion.5), channel_id=1, source_target_pairs={{0,8},{8,0},{16,24},{24,16},{1,9},{9,1},{17,25},{25,17},{2,10},{10... | collective-permute-start | bytes 8650760 | tf_op jit(solution)/shard_map/ppermute | solution.py:600
  (158 other events, 5133.7 us)
Sparse Core Ops, SparseCore 0:
  32.3 116.8 all-gather.6
  151.3 113.5 all-gather.8
  339.8 108.8 reduce-scatter.4
  457.8 111.7 all-gather.10
  967.1 120.0 reduce-scatter.6
  1101.0 123.8 all-gather.12
  1237.6 118.0 reduce-scatter.8
  1432.7 107.0 reduce-scatter.10

commit v2 on v1

--- a/solution.py
+++ b/solution.py
@@ -790,7 +790,19 @@
     lead_held = lead.over_dp(lead_held, 1)
     qkv_all = whole(flat_qkv, 0, lead_held[0])
     out_all = whole(w_out, 1, lead_held[1])
-    n1, dy_part, qkv_all, out_all = lax.optimization_barrier((n1, dy_part, qkv_all, out_all))
+    block = 256 if rows % 256 == 0 else 128
+    shape = (rows // block, block, depth)
+    take = lambda v: lax.dynamic_index_in_dim(
+        v.reshape(groups, parts, size, v.shape[1]), gy, 1, keepdims=False
+    ).reshape(rows, v.shape[1])
+    flip = (1 - (dp & 1)) * (E // 2)
+    plan = plan_tiles(take(routes) ^ flip, take(route_weights), block)
+    spot = jnp.stack([dp, flip]).astype(jnp.int32)
+    tables = {name: table for name, table in plan.items() if name not in ("room", "number")}
+    n1, dy_part, qkv_all, out_all, early_held[2:], tables = lax.optimization_barrier(
+        (n1, dy_part, qkv_all, out_all, early_held[2:], tables)
+    )
+    plan |= tables
     dy = gather_rows(dy_part)
 
     q, kv = project_qkv(n1, qkv_all, qkv_bias, cos, sin)
@@ -803,23 +815,15 @@
     shared_held = early.over_dp(shared_held, 0)
     up_held = late[0].over_gy(tie(late[0].cut(), kv_rest))
     o, o_exact, level = attend(span, q, kv, kv_rest, size, parts, count)
-    o, up_held, shared_held = lax.optimization_barrier((o, up_held, shared_held))
+    o, shared_held = lax.optimization_barrier((o, shared_held))
     attn_part = dot(o, out_all).astype(BF16)
-    attn_part, dy = lax.optimization_barrier((attn_part, dy))
+    attn_part, dy, up_held = lax.optimization_barrier((attn_part, dy, up_held))
     attn = sum_rows(attn_part).astype(F32)
-    down_held = late[1].over_gy(tie(late[1].cut(), o))
+    down_held = late[1].over_gy(tie(late[1].cut(), attn_part))
     shared_held = early.over_dp(shared_held, 1)
     gate_held = early.over_dp(gate_held, 1)
     up_held = late[0].over_dp(up_held, 0)
 
-    block = 256 if rows % 256 == 0 else 128
-    shape = (rows // block, block, depth)
-    take = lambda v: lax.dynamic_index_in_dim(
-        v.reshape(groups, parts, size, v.shape[1]), gy, 1, keepdims=False
-    ).reshape(rows, v.shape[1])
-    flip = (1 - (dp & 1)) * (E // 2)
-    plan = plan_tiles(take(routes) ^ flip, take(route_weights), block)
-    spot = jnp.stack([dp, flip]).astype(jnp.int32)
     d_slots = send_out(plan, dy.reshape(shape), True)
     sg_all = whole(shared_gate, 0, shared_held[0])
     su_all = whole(shared_up, 0, shared_held[1])
@@ -831,8 +835,8 @@
     inv_ffn = lax.rsqrt(jnp.mean(middle * middle, axis=1, keepdims=True) + EPS)
     unit_ffn = middle * inv_ffn
     n2_part = (unit_ffn * gain_ffn).astype(BF16)
-    n2_part, up_held, down_held, d_slots, d_s_hidden, plan["halves"] = lax.optimization_barrier(
-        (n2_part, up_held, down_held, d_slots, d_s_hidden, plan["halves"])
+    n2_part, up_held, down_held, d_slots, d_s_hidden = lax.optimization_barrier(
+        (n2_part, up_held, down_held, d_slots, d_s_hidden)
     )
     n2 = gather_rows(n2_part)
     up_held = late[0].over_dp(up_held, 1)
@@ -935,16 +939,24 @@
     gu_sums[2] = reduce.over_gy(gu_sums[2])
     d_mixed, bias_part = mix_back(dq, dkv_own, got, cos, sin)
     d_n1_part = dot(d_mixed, qkv_all, cols).astype(BF16)
+    d_n1_part, d_mixed, branch = lax.optimization_barrier((d_n1_part, d_mixed, branch))
     d_n1 = sum_rows(d_n1_part).astype(F32)
-    d_mixed = tie(d_mixed, d_n1_part)
+    result = middle + branch
     qkv_sums = reduce.near([[dot(a, d_mixed, both).astype(BF16) for a in split_blocks(n1, parts, 1)]])
-    attn_sums = reduce.over_gy(qkv_sums + out_sums)
+    attn_sums = qkv_sums + out_sums
+    attn_sums, gu_sums[1:] = lax.optimization_barrier((attn_sums, gu_sums[1:]))
     gu_sums[2] = reduce.over_dp(gu_sums[2])
+    attn_sums = reduce.over_gy(attn_sums)
+    attn_sums, d_n1 = lax.optimization_barrier((attn_sums, d_n1))
     grad_w_qkv, grad_w_out = reduce.finish(reduce.over_dp(attn_sums))
     grad_w_qkv = grad_w_qkv.reshape(width, heads, 3 * HD)
-    result = middle + branch
-
-    sums = jnp.stack([gain_ffn_part, router_part])
+    gain_attn_part = jnp.sum(d_n1 * unit_attn, axis=0)
+    scaled = d_n1 * gain_attn
+    grad_stream = d_middle + inv_attn * (
+        scaled - unit_attn * jnp.mean(scaled * unit_attn, axis=1, keepdims=True)
+    )
+
+    sums = jnp.stack([gain_attn_part, gain_ffn_part, router_part])
     sums = lax.dynamic_slice_in_dim(
         jnp.concatenate([sums, sums], axis=1), ((parts - gy) % parts) * width, depth, axis=1
     )
@@ -955,57 +967,44 @@
     squares = jnp.stack(
         [jnp.sum(valid * v * v) for v in (middle, result, attn, branch)] + [jnp.sum(valid) * depth]
     )
-    sums = tie(jnp.concatenate([sums.reshape(-1), biases, squares]), d_n1_part)
-    sums = lax.psum(sums, ("dp", "gx", "gy"))
-    d_n1, sums = lax.optimization_barrier((d_n1, sums))
+    sums = lax.psum(jnp.concatenate([sums.reshape(-1), biases, squares]), ("dp", "gx", "gy"))
+    vectors = lax.dynamic_slice_in_dim(sums[: 3 * depth].reshape(3, depth), gy * width, width, axis=1)
+    bias_sum = lax.dynamic_slice_in_dim(sums[3 * depth : -5], gx * heads * 3 * HD, heads * 3 * HD)
+    bias_sum = bias_sum.reshape(heads, 3 * HD)
+    grad_columns = to_columns(grad_stream, F32)
     hidden = gate_t.shape[1]
     gu = [gu_sum for [gu_sum] in gu_sums]
+    gu[2], grad_columns = lax.optimization_barrier((gu[2], grad_columns))
     gu_other = [across(v, 1) for v in gu]
     side = dp & 1
     grad_gate, grad_up = (
         jnp.swapaxes(
             jnp.concatenate(
-                [jnp.where(side == 0, a[:, part], b[:, part]) for a, b in zip(gu, gu_other)]
-                + [jnp.where(side == 0, b[:, part], a[:, part]) for a, b in zip(gu, gu_other)],
+                [jnp.where(side == 0, a[:, part], b[:, part]).astype(F32) for a, b in zip(gu, gu_other)]
+                + [jnp.where(side == 0, b[:, part], a[:, part]).astype(F32) for a, b in zip(gu, gu_other)],
                 axis=0,
-            ).astype(F32),
+            ),
             1,
             2,
         )
         for part in (slice(0, hidden), slice(hidden, 2 * hidden))
     )
-    gain_attn_part = jnp.sum(d_n1 * unit_attn, axis=0)
-    scaled = d_n1 * gain_attn
-    grad_stream = d_middle + inv_attn * (
-        scaled - unit_attn * jnp.mean(scaled * unit_attn, axis=1, keepdims=True)
-    )
-
-    def added(vectors):
-        own, *rest = split_blocks(vectors, parts, 1)
-        for k, piece in enumerate(rest, start=1):
-            own = own + from_ahead(piece, parts - k)
-        return jnp.sum(lax.all_gather(own, ("dp", "gx")), axis=0)
-
-    [gain_sum] = added(gain_attn_part[None])
-    vectors = lax.dynamic_slice_in_dim(sums[: 2 * depth].reshape(2, depth), gy * width, width, axis=1)
-    bias_sum = lax.dynamic_slice_in_dim(sums[2 * depth : -5], gx * flat_bias.shape[0], flat_bias.shape[0])
-    bias_sum = bias_sum.reshape(heads, 3 * HD)
     rms_stats = jnp.sqrt(sums[-5:-1] / sums[-1])
     return (
         to_columns(result, BF16),
-        to_columns(grad_stream, F32),
-        gain_sum,
+        grad_columns,
+        vectors[0],
         grad_w_qkv,
         bias_sum,
         grad_w_out,
-        vectors[0],
+        vectors[1],
         grad_gate,
         grad_up,
         grad_down,
         grad_sgate,
         grad_sup,
         grad_sdown,
-        vectors[1],
+        vectors[2],
         rms_stats,
     )
 

time: 1860 us -> 1780 us (0.957); the launches traced: 1840 us -> 1780 us
  starting transfers between devices: 105 us -> 67.4 us
  waiting for transfers between devices: 556 us -> 534 us
    ppermute x56, starting transfers between devices: 74.7 us -> 31.7 us  [across(): return lax.ppermute(values, 'dp', [(d, d ^ bit) for d in range(n)])]
    ppermute x56, waiting for transfers between devices: 400 us -> 364 us  [across(): return lax.ppermute(values, 'dp', [(d, d ^ bit) for d in range(n)])]
    all_gather x1 -> x0, blocking collectives: 31.7 us -> none  [added(): return jnp.sum(lax.all_gather(own, ('dp', 'gx')), axis=0)]
    psum x1, blocking collectives: 37.3 us -> 67 us  [local(): lax.psum(jnp.concatenate([sums.reshape(-1), biases, squares]), ('dp', 'gx...]
    ppermute x25 -> x24, waiting for transfers between devices: 115 us -> 127 us  [from_ahead(): return lax.ppermute(values, 'gy', [(s, (s - shift) % n) for s in range(n)])]
    unnamed x28 -> x23, other arithmetic: 51.1 us -> 51.1 us
  transfers between devices with their start and end apart: 89 -> 88, of which waited for: 23 -> 20; matrix products, arithmetic and copies ran while one was open for 32% -> 31% of each run, Pallas kernels for 14% -> 15%
where the time goes in v2:
time: 1780 us
  waiting for transfers between devices  534 us (30%)
  Pallas kernels  408 us (23%)
  other arithmetic  382 us (21%)
  matrix products  206 us (12%)
  local copies, waits for them, and re-layouts  92.6 us (5%)
  starting transfers between devices  67.4 us (4%)
  blocking collectives  67 us (4%)
  between operations  17.9 us (1%)
    ppermute x56, waiting for transfers between devices, across(): return lax.ppermute(values, 'dp', [(d, d ^ bit) for d in range(n)])  364 us
    pallas_call x2, Pallas kernels, experts(): pl.pallas_call(functools.partial(experts_body, (cut, number, hidden, half...  210 us
    dot_general x19, matrix products, dot(): return lax.dot_general(a, b, (dims, ((), ())), preferred_element_type=F32)  206 us
    ppermute x24, waiting for transfers between devices, from_ahead(): return lax.ppermute(values, 'gy', [(s, (s - shift) % n) for s in range(n)])  127 us
    psum x1, blocking collectives, local(): lax.psum(jnp.concatenate([sums.reshape(-1), biases, squares]), ('dp', 'gx...  67 us
    unnamed x23, other arithmetic  51.1 us
    pallas_call x1, Pallas kernels, attend_back(): pl.pallas_call(functools.partial(attend_back_body, (size, blocks, parts,...  47.3 us
    pallas_call x2, Pallas kernels, bring_back(): pl.pallas_call(functools.partial(bring_back_body, (blocks, top, room, wei...  46.1 us
  transfers between devices with their start and end apart: 88, of which 20 were waited for; matrix products, arithmetic and copies ran while one was open for 31% of the time, Pallas kernels for 15%

profile of v2, /device:TPU:0, one launch (start us, length us, event | category | flops | bytes accessed | tf_op | source)
XLA Modules:
  0.0 1775.9 jit_solution(2523749104601572712)
XLA Ops:
  21.7 34.1 %collective-permute-done.1 = bf16[3,1024]{1,0:T(4,128)(2,1)S(1)} collective-permute-done((bf16[3,1024]{1,0:T(4,128)(2,1)S(1)}, bf16[3,1024]{1,0:T(4,128)(2,1)S(1)}, u32[]{:S(2)}, u32[]{:S(2)}) %collective-permute-start.1) | collective-permute-done | bytes 6176 | tf_op jit(solution)/shard_map/ppermute | solution.py:595
  131.1 18.2 %collective-permute-done.11 = bf16[352,1024]{1,0:T(8,128)(2,1)} collective-permute-done((bf16[352,1024]{1,0:T(8,128)(2,1)}, bf16[352,1024]{1,0:T(8,128)(2,1)}, u32[]{:S(2)}, u32[]{:S(2)}) %collective-permute-start.11) | collective-permute-done | bytes 720928 | tf_op jit(solution)/shard_map/ppermute | solution.py:595
  149.2 26.8 %all-gather.5.cloned.1.call-done.n1 = bf16[1536,2048]{1,0:T(8,128)(2,1)} async-done(((bf16[384,2048]{1,0:T(8,128)(2,1)}), bf16[1536,2048]{1,0:T(8,128)(2,1)}) %all-gather.5.cloned.1.call-update) | async-done | bytes 6291472 | tf_op jit(solution)/shard_map/all_gather | solution.py:730
  184.9 19.5 %project_qkv.1 = (bf16[1536,512]{1,0:T(8,128)(2,1)}, bf16[1536,1024]{1,0:T(8,128)(2,1)}) custom-call(bf16[1536,2048]{1,0:T(8,128)(2,1)} %all-gather.5.cloned.1.call-done.n1, bf16[2048,1536]{1,0:T(8,128)(2,1)} %select_dynamic-update-slice_fusion.12.w, bf16[4,1,384]{2,1,0:T(2,128)(2,1)} %copy.118.bias, f32[1536,128]{1,0:T(8,128)} %get-tuple-element.419.cos.refs_1_, ...), custom_call_target="tpu_custom_call" | custom-call | flops 9663676416 | bytes 12582912 | tf_op jit(solution)/shard_map/project_qkv/pallas_call | solution.py:59
  213.3 62.3 %collective-permute-done.16 = bf16[4,352,1024]{2,1,0:T(8,128)(2,1)} collective-permute-done((bf16[4,352,1024]{2,1,0:T(8,128)(2,1)}, bf16[4,352,1024]{2,1,0:T(8,128)(2,1)}, u32[]{:S(2)}, u32[]{:S(2)}) %collective-permute-start.16) | collective-permute-done | bytes 2883616 | tf_op jit(solution)/shard_map/ppermute | solution.py:600
  285.6 43.8 %attend.1 = (bf16[1536,512]{1,0:T(8,128)(2,1)}, f32[1536,512]{1,0:T(8,128)}, f32[1536,512]{1,0:T(8,128)}) custom-call(s32[3]{0:T(128)} %pad_add_fusion.meta, bf16[1536,512]{1,0:T(8,128)(2,1)} %get-tuple-element.163.q, bf16[1536,1024]{1,0:T(8,128)(2,1)} %get-tuple-element.169.kv_own, bf16[1536,1024]{1,0:T(8,128)(2,1)} %collective-permute-done.15.kv_rem), custom_call_target="tpu_custom_call" | custom-call | flops 14495514624 | bytes 23592960 | tf_op jit(solution)/shard_map/attend/pallas_call | solution.py:162
  353.1 24.3 %pad_maximum_fusion.gu_own = bf16[16,704,1024]{2,1,0:T(8,128)(2,1)} fusion(bf16[16,352,1024]{2,1,0:T(8,128)(2,1)} %bitcast.133, bf16[16,352,1024]{2,1,0:T(8,128)(2,1)} %bitcast.134), kind=kLoop, calls=%fused_computation | loop fusion | flops 46137344 | bytes 46137344 | tf_op jit(solution)/shard_map/concatenate | solution.py:847
  387.4 31.1 %fusion.85 = f32[1536,1408]{1,0:T(8,128)} fusion(bf16[1536,2048]{1,0:T(8,128)(2,1)} %all-gather.7.cloned.1.call-done, bf16[352,1024]{1,0:T(8,128)(2,1)S(1)} %get-tuple-element.370, bf16[352,1024]{1,0:T(8,128)(2,1)S(1)} %get-tuple-element.369, bf16[352,1024]{1,0:T(8,128)(2,1)S(1)} %get-tuple-element.368, bf16[352,1024]{1,0:T(8,128)(2,1)S(1)} %get-tuple-element.367, ...), kind=kOutput, calls=%fused_computation.351 | convolution fusion | flops 8887205888 | bytes 20709376 | tf_op jit(solution)/shard_map/dot_general | solution.py:27
  418.5 17.7 send_out.2
  436.2 15.9 reduce-scatter.5.cloned.1.call-done
  478.3 51.1 %collective-permute-done.30 = bf16[4,352,1024]{2,1,0:T(8,128)(2,1)S(1)} collective-permute-done((bf16[4,352,1024]{2,1,0:T(8,128)(2,1)}, bf16[4,352,1024]{2,1,0:T(8,128)(2,1)S(1)}, u32[]{:S(2)}, u32[]{:S(2)}) %collective-permute-start.30) | collective-permute-done | bytes 2883616 | tf_op jit(solution)/shard_map/ppermute | solution.py:600
  529.5 37.8 %maximum_maximum_fusion.gu_rem = bf16[16,704,1024]{2,1,0:T(8,128)(2,1)} fusion(bf16[4,352,1024]{2,1,0:T(8,128)(2,1)S(1)} %collective-permute-done.28, bf16[4,352,1024]{2,1,0:T(8,128)(2,1)S(1)} %collective-permute-done.27, bf16[4,352,1024]{2,1,0:T(8,128)(2,1)} %collective-permute-done.21, bf16[4,352,1024]{2,1,0:T(8,128)(2,1)} %collective-permute-done.16, ...), kind=kLoop, calls=%fused_computation.1 | loop fusion | flops 184549376 | bytes 46137344 | tf_op jit(solution)/shard_map/concatenate | solution.py:848
  574.8 15.1 send_out.3
  589.9 99.6 %experts_first.1 = (bf16[11520,2048]{1,0:T(8,128)(2,1)}, bf16[11520,2048]{1,0:T(8,128)(2,1)}, bf16[8,704,1024]{2,1,0:T(8,128)(2,1)}, bf16[8,704,1024]{2,1,0:T(8,...) custom-call(s32[6,34]{1,0:T(8,128)} %stack.59.meta, s32[34,16]{1,0:T(8,128)} %copy.122.source, ...), custom_call_target="tpu_custom_call" | custom-call | flops 74742497280 | bytes 140509184 | tf_op jit(solution)/shard_map/experts_first/pallas_call | solution.py:570
  689.5 15.4 fusion.95
  706.3 19.8 %multiply_reduce_fusion = (f32[1536]{0:T(1024)S(1)}, bf16[1536,1408]{1,0:T(8,128)(2,1)}, bf16[1536,1408]{1,0:T(8,128)(2,1)}, bf16[1536,1408]{1,0:T(8,128)(2,1)}) fusion(f32[1536,1408]{1,0:T(8,128)} %fusion.85, f32[1536,1408]{1,0:T(8,128)} %fusion.95, f32[1536]{0:T(1024)S(1)} %add_divide_fusion.1, bf16[1536,2048]{1,0:T(8,128)(2,1)S(1)} %bitcast.124, ...), kind=kOutput, calls=%fused_computation.19 | convolution fusion | flops 8901621760 | bytes 42348544 | tf_op jit(solution)/shard_map/dot_general | solution.py:27
  772.3 16.9 add_convert_fusion
  830.2 110.4 %experts_second.1 = (bf16[11520,2048]{1,0:T(8,128)(2,1)}, bf16[11520,2048]{1,0:T(8,128)(2,1)}, bf16[8,704,1024]{2,1,0:T(8,128)(2,1)}, bf16[8,704,1024]{2,1,0:T(8...) custom-call(s32[6,34]{1,0:T(8,128)} %stack.61.meta, ...), custom_call_target="tpu_custom_call", output_to_operand_aliasing={{0}: (13, {}), {1}: (14, {})} | custom-call | flops 74742497280 | bytes 140509184 | tf_op jit(solution)/shard_map/experts_second/pallas_call | solution.py:570
  947.3 22.0 %bring_back.2 = bf16[6,256,2048]{2,1,0:T(8,128)(2,1)} custom-call(s32[6,79]{1,0:T(8,128)} %select_reduce_fusion.3.get, s32[6,256,4]{2,1,0:T(8,128)} %bitcast.137, bf16[11520,2048]{1,0:T(8,128)(2,1)} %get-tuple-element.235.refs_0_), custom_call_target="tpu_custom_call" | custom-call | flops 7952400384 | bytes 62128128 | tf_op jit(solution)/shard_map/bring_back/pallas_call | solution.py:464
  986.7 24.1 %bring_back.3 = bf16[6,256,2048]{2,1,0:T(8,128)(2,1)} custom-call(s32[6,79]{1,0:T(8,128)} %select_reduce_fusion.3.get, s32[6,256,4]{2,1,0:T(8,128)} %bitcast.138, f32[6,256,4]{2,1,0:T(8,128)} %bitcast.143, bf16[11520,2048]{1,0:T(8,128)(2,1)} %get-tuple-element.241.refs_1_), custom_call_target="tpu_custom_call" | custom-call | flops 7952400384 | bytes 62128128 | tf_op jit(solution)/shard_map/bring_back/pallas_call | solution.py:464
  1010.8 17.4 fusion.2
  1053.2 21.9 %collective-permute-done.50 = bf16[512,1408]{1,0:T(8,128)(2,1)} collective-permute-done((bf16[512,1408]{1,0:T(8,128)(2,1)}, bf16[512,1408]{1,0:T(8,128)(2,1)}, u32[]{:S(2)}, u32[]{:S(2)}) %collective-permute-start.50) | collective-permute-done | bytes 1441824 | tf_op jit(solution)/shard_map/ppermute | solution.py:600
  1078.0 23.7 %collective-permute-done.49 = bf16[8,352,1024]{2,1,0:T(8,128)(2,1)} collective-permute-done((bf16[8,352,1024]{2,1,0:T(8,128)(2,1)}, bf16[8,352,1024]{2,1,0:T(8,128)(2,1)}, u32[]{:S(2)}, u32[]{:S(2)}) %collective-permute-start.49) | collective-permute-done | bytes 5767200 | tf_op jit(solution)/shard_map/ppermute | solution.py:595
  1123.7 122.5 %collective-permute-done.54 = bf16[8,352,1024]{2,1,0:T(8,128)(2,1)} collective-permute-done((bf16[8,352,1024]{2,1,0:T(8,128)(2,1)}, bf16[8,352,1024]{2,1,0:T(8,128)(2,1)}, u32[]{:S(2)}, u32[]{:S(2)}) %collective-permute-start.54) | collective-permute-done | bytes 5767200 | tf_op jit(solution)/shard_map/ppermute | solution.py:600
  1274.6 47.3 %attend_back.1 = (bf16[1536,512]{1,0:T(8,128)(2,1)}, f32[1536,1024]{1,0:T(8,128)}, bf16[1536,1024]{1,0:T(8,128)(2,1)}) custom-call(s32[3]{0:T(128)} %pad_add_fusion.meta, bf16[1536,512]{1,0:T(8,128)(2,1)} %get-tuple-element.163.q, bf16[1536,1024]{1,0:T(8,128)(2,1)} %get-tuple-element.169.kv_own, bf16[1536,1024]{1,0:T(8,128)(2,1)} %collective-permute-done.15.kv_rem, ...), custom_call_target="tpu_custom_call" | custom-call | flops 24159191040 | bytes 31457280 | tf_op jit(solution)/shard_map/attend_back/pallas_call | solution.py:245
  1349.9 38.7 %collective-permute-done.59 = bf16[4,704,1024]{2,1,0:T(8,128)(2,1)} collective-permute-done((bf16[4,704,1024]{2,1,0:T(8,128)(2,1)}, bf16[4,704,1024]{2,1,0:T(8,128)(2,1)}, u32[]{:S(2)}, u32[]{:S(2)}) %collective-permute-start.59) | collective-permute-done | bytes 5767200 | tf_op jit(solution)/shard_map/ppermute | solution.py:600
  1408.4 15.6 convolution_convert_fusion
  1476.0 37.4 %collective-permute-done.63 = bf16[2,704,1024]{2,1,0:T(8,128)(2,1)} collective-permute-done((bf16[2,704,1024]{2,1,0:T(8,128)(2,1)}, bf16[2,704,1024]{2,1,0:T(8,128)(2,1)}, u32[]{:S(2)}, u32[]{:S(2)}) %collective-permute-start.63) | collective-permute-done | bytes 2883616 | tf_op jit(solution)/shard_map/ppermute | solution.py:600
  1549.4 27.8 %collective-permute-done.67 = bf16[256,1024]{1,0:T(8,128)(2,1)S(1)} collective-permute-done((bf16[256,1024]{1,0:T(8,128)(2,1)}, bf16[256,1024]{1,0:T(8,128)(2,1)S(1)}, u32[]{:S(2)}, u32[]{:S(2)}) %collective-permute-start.67) | collective-permute-done | bytes 524320 | tf_op jit(solution)/shard_map/ppermute | solution.py:595
  1600.3 13.8 collective-permute-done.65
  1625.4 67.0 %psum.7 = f32[12293]{0:T(1024)S(1)} all-reduce(f32[12293]{0:T(1024)S(1)} %concatenate.141), channel_id=1, replica_groups=mesh['dp'=4,'gx'=4,'gy'=2] {'dp','gx','gy'}, use_global_device_ids=true, to_apply=%region_45.46 | all-reduce | flops 12293 | bytes 98344 | tf_op jit(solution)/shard_map/psum | solution.py:970
  1744.6 13.8 convert_bitcast_fusion
  (585 shorter events, 604.9 us)
Async XLA Ops:
  7.2 168.8 %all-gather.5.cloned.1.call-start = ((), (), s32[]{:S(2)}) async-start(), calls=%async_computation.4 | async-start | bytes 7864320 | tf_op jit(solution)/shard_map/all_gather | solution.py:730
  11.8 72.7 %collective-permute-start.7 = (bf16[128,1024]{1,0:T(8,128)(2,1)S(1)}, bf16[128,1024]{1,0:T(8,128)(2,1)}, u32[]{:S(2)}, u32[]{:S(2)}) collective-permute-start(bf16[128,1024]{1,0:T(8,128)(2,1)S(1)} %constant_dynamic-slice_fusion.16), channel_id=1, source_target_pairs={{0,1},{1,0},{2,3},{3,2},{4,5},{5,4},{6,7},{7,6},{8,9},{9,8},{10,11... | collective-permute-start | bytes 786440 | tf_op jit(solution)/shard_map/ppermute | solution.py:595
  19.8 98.5 %collective-permute-start.2 = (bf16[384,1024]{1,0:T(8,128)(2,1)}, bf16[384,1024]{1,0:T(8,128)(2,1)}, u32[]{:S(2)}, u32[]{:S(2)}) collective-permute-start(bf16[384,1024]{1,0:T(8,128)(2,1)} %get-tuple-element.374), channel_id=1, source_target_pairs={{0,1},{1,0},{2,3},{3,2},{4,5},{5,4},{6,7},{7,6},{8,9},{9,8},{10,11... | collective-permute-start | bytes 2359304 | tf_op jit(solution)/shard_map/ppermute | solution.py:595
  58.7 284.4 %all-gather.7.cloned.1.call-start = ((), (), s32[]{:S(2)}) async-start(), calls=%async_computation.5 | async-start | bytes 7864320 | tf_op jit(solution)/shard_map/all_gather | solution.py:730
  69.5 79.7 %collective-permute-start.12 = (bf16[4,352,1024]{2,1,0:T(8,128)(2,1)}, bf16[4,352,1024]{2,1,0:T(8,128)(2,1)}, u32[]{:S(2)}, u32[]{:S(2)}) collective-permute-start(bf16[4,352,1024]{2,1,0:T(8,128)(2,1)} %get-tuple-element.160), channel_id=1, source_target_pairs={{0,1},{1,0},{2,3},{3,2},{4,5},{5,4},{6,7},{7,6},{8,9},{9,8},{10,11... | collective-permute-start | bytes 8650760 | tf_op jit(solution)/shard_map/ppermute | solution.py:595
  176.0 276.1 %reduce-scatter.5.cloned.1.call-start = ((), (), s32[]{:S(2)}) async-start(), calls=%async_computation.6 | async-start | bytes 7864320 | tf_op jit(solution)/shard_map/reduce_scatter | solution.py:734
  343.1 231.7 %all-gather.9.cloned.1.call-start = ((), (), s32[]{:S(2)}) async-start(), calls=%async_computation.7 | async-start | bytes 7864320 | tf_op jit(solution)/shard_map/all_gather | solution.py:730
  381.7 75.1 %collective-permute-start.32 = (bf16[256,1408]{1,0:T(8,128)(2,1)}, bf16[256,1408]{1,0:T(8,128)(2,1)}, u32[]{:S(2)}, u32[]{:S(2)}) collective-permute-start(bf16[256,1408]{1,0:T(8,128)(2,1)} %collective-permute-done.18), channel_id=1, source_target_pairs={{0,8},{8,0},{16,24},{24,16},{1,9},{9,1},{17,25},{25,17},{2,10},{10... | collective-permute-start | bytes 2162696 | tf_op jit(solution)/shard_map/ppermute | solution.py:600
  381.7 75.3 %collective-permute-start.33 = (bf16[256,1408]{1,0:T(8,128)(2,1)}, bf16[256,1408]{1,0:T(8,128)(2,1)}, u32[]{:S(2)}, u32[]{:S(2)}) collective-permute-start(bf16[256,1408]{1,0:T(8,128)(2,1)} %copy-done.18), channel_id=1, source_target_pairs={{0,8},{8,0},{16,24},{24,16},{1,9},{9,1},{17,25},{25,17},{2,10},{10... | collective-permute-start | bytes 2162696 | tf_op jit(solution)/shard_map/ppermute | solution.py:600
  382.2 83.5 %collective-permute-start.34 = (bf16[256,1408]{1,0:T(8,128)(2,1)}, bf16[256,1408]{1,0:T(8,128)(2,1)}, u32[]{:S(2)}, u32[]{:S(2)}) collective-permute-start(bf16[256,1408]{1,0:T(8,128)(2,1)} %collective-permute-done.17), channel_id=1, source_target_pairs={{0,8},{8,0},{16,24},{24,16},{1,9},{9,1},{17,25},{25,17},{2,10},{10... | collective-permute-start | bytes 2162696 | tf_op jit(solution)/shard_map/ppermute | solution.py:600
  456.8 653.1 %reduce-scatter.7.cloned.1.call-start = ((), (), s32[]{:S(2)}) async-start(), calls=%async_computation.8 | async-start | bytes 7864320 | tf_op jit(solution)/shard_map/reduce_scatter | solution.py:734
  456.8 72.6 %collective-permute-start.27 = (bf16[4,352,1024]{2,1,0:T(8,128)(2,1)}, bf16[4,352,1024]{2,1,0:T(8,128)(2,1)S(1)}, u32[]{:S(2)}, u32[]{:S(2)}) collective-permute-start(bf16[4,352,1024]{2,1,0:T(8,128)(2,1)} %collective-permute-done.16), channel_id=1, source_target_pairs={{0,8},{8,0},{16,24},{24,16},{1,9},{9,1},{17,25},{25,17},{2,10},{10... | collective-permute-start | bytes 8650760 | tf_op jit(solution)/shard_map/ppermute | solution.py:600
  478.2 89.1 %collective-permute-start.29 = (bf16[4,352,1024]{2,1,0:T(8,128)(2,1)}, bf16[4,352,1024]{2,1,0:T(8,128)(2,1)S(1)}, u32[]{:S(2)}, u32[]{:S(2)}) collective-permute-start(bf16[4,352,1024]{2,1,0:T(8,128)(2,1)} %collective-permute-done.22), channel_id=1, source_target_pairs={{0,8},{8,0},{16,24},{24,16},{1,9},{9,1},{17,25},{25,17},{2,10},{10... | collective-permute-start | bytes 8650760 | tf_op jit(solution)/shard_map/ppermute | solution.py:600
  741.9 80.3 %collective-permute-start.42 = (bf16[8,704,1024]{2,1,0:T(8,128)(2,1)}, bf16[8,704,1024]{2,1,0:T(8,128)(2,1)}, u32[]{:S(2)}, u32[]{:S(2)}) collective-permute-start(bf16[8,704,1024]{2,1,0:T(8,128)(2,1)} %get-tuple-element.206), channel_id=1, source_target_pairs={{0,8},{8,0},{16,24},{24,16},{1,9},{9,1},{17,25},{25,17},{2,10},{10... | collective-permute-start | bytes 34603016 | tf_op jit(solution)/shard_map/ppermute | solution.py:600
  742.0 80.2 %collective-permute-start.43 = (bf16[8,704,1024]{2,1,0:T(8,128)(2,1)}, bf16[8,704,1024]{2,1,0:T(8,128)(2,1)}, u32[]{:S(2)}, u32[]{:S(2)}) collective-permute-start(bf16[8,704,1024]{2,1,0:T(8,128)(2,1)} %get-tuple-element.207), channel_id=1, source_target_pairs={{0,8},{8,0},{16,24},{24,16},{1,9},{9,1},{17,25},{25,17},{2,10},{10... | collective-permute-start | bytes 34603016 | tf_op jit(solution)/shard_map/ppermute | solution.py:600
  822.2 118.4 %collective-permute-start.48 = (bf16[704,1024]{1,0:T(8,128)(2,1)S(1)}, bf16[704,1024]{1,0:T(8,128)(2,1)}, u32[]{:S(2)}, u32[]{:S(2)}) collective-permute-start(bf16[704,1024]{1,0:T(8,128)(2,1)S(1)} %add_convert_fusion.19), channel_id=1, source_target_pairs={{0,1},{1,0},{2,3},{3,2},{4,5},{5,4},{6,7},{7,6},{8,9},{9,8},{10,11... | collective-permute-start | bytes 4325384 | tf_op jit(solution)/shard_map/ppermute | solution.py:595
  828.1 114.5 %collective-permute-start.47 = (bf16[512,1408]{1,0:T(8,128)(2,1)}, bf16[512,1408]{1,0:T(8,128)(2,1)}, u32[]{:S(2)}, u32[]{:S(2)}) collective-permute-start(bf16[512,1408]{1,0:T(8,128)(2,1)} %add_convert_fusion.21), channel_id=1, source_target_pairs={{0,1},{1,0},{2,3},{3,2},{4,5},{5,4},{6,7},{7,6},{8,9},{9,8},{10,11... | collective-permute-start | bytes 4325384 | tf_op jit(solution)/shard_map/ppermute | solution.py:595
  828.2 116.3 %collective-permute-start.46 = (bf16[512,1408]{1,0:T(8,128)(2,1)}, bf16[512,1408]{1,0:T(8,128)(2,1)}, u32[]{:S(2)}, u32[]{:S(2)}) collective-permute-start(bf16[512,1408]{1,0:T(8,128)(2,1)} %add_convert_fusion.23), channel_id=1, source_target_pairs={{0,1},{1,0},{2,3},{3,2},{4,5},{5,4},{6,7},{7,6},{8,9},{9,8},{10,11... | collective-permute-start | bytes 4325384 | tf_op jit(solution)/shard_map/ppermute | solution.py:595
  980.4 284.2 %all-gather.11.cloned.1.call-start = ((), (), s32[]{:S(2)}) async-start(), calls=%async_computation.9 | async-start | bytes 7864320 | tf_op jit(solution)/shard_map/all_gather | solution.py:730
  980.5 121.2 %collective-permute-start.49 = (bf16[8,352,1024]{2,1,0:T(8,128)(2,1)}, bf16[8,352,1024]{2,1,0:T(8,128)(2,1)}, u32[]{:S(2)}, u32[]{:S(2)}) collective-permute-start(bf16[8,352,1024]{2,1,0:T(8,128)(2,1)} %get-tuple-element.238), channel_id=1, source_target_pairs={{0,1},{1,0},{2,3},{3,2},{4,5},{5,4},{6,7},{7,6},{8,9},{9,8},{10,11... | collective-permute-start | bytes 17301512 | tf_op jit(solution)/shard_map/ppermute | solution.py:595
  986.7 88.4 %collective-permute-start.50 = (bf16[512,1408]{1,0:T(8,128)(2,1)}, bf16[512,1408]{1,0:T(8,128)(2,1)}, u32[]{:S(2)}, u32[]{:S(2)}) collective-permute-start(bf16[512,1408]{1,0:T(8,128)(2,1)} %add_convert_fusion.18), channel_id=1, source_target_pairs={{0,16},{8,24},{16,0},{24,8},{1,17},{9,25},{17,1},{25,9},{2,18},{10... | collective-permute-start | bytes 4325384 | tf_op jit(solution)/shard_map/ppermute | solution.py:600
  1117.0 307.1 %reduce-scatter.9.cloned.1.call-start = ((), (), s32[]{:S(2)}) async-start(), calls=%async_computation.10 | async-start | bytes 7864320 | tf_op jit(solution)/shard_map/reduce_scatter | solution.py:734
  1117.2 129.0 %collective-permute-start.54 = (bf16[8,352,1024]{2,1,0:T(8,128)(2,1)}, bf16[8,352,1024]{2,1,0:T(8,128)(2,1)}, u32[]{:S(2)}, u32[]{:S(2)}) collective-permute-start(bf16[8,352,1024]{2,1,0:T(8,128)(2,1)} %add_convert_fusion.4), channel_id=1, source_target_pairs={{0,16},{8,24},{16,0},{24,8},{1,17},{9,25},{17,1},{25,9},{2,18},{10... | collective-permute-start | bytes 17301512 | tf_op jit(solution)/shard_map/ppermute | solution.py:600
  1123.4 132.9 %collective-permute-start.53 = (bf16[4,704,1024]{2,1,0:T(8,128)(2,1)}, bf16[4,704,1024]{2,1,0:T(8,128)(2,1)S(1)}, u32[]{:S(2)}, u32[]{:S(2)}) collective-permute-start(bf16[4,704,1024]{2,1,0:T(8,128)(2,1)} %slice.165), channel_id=1, source_target_pairs={{0,1},{1,0},{2,3},{3,2},{4,5},{5,4},{6,7},{7,6},{8,9},{9,8},{10,11... | collective-permute-start | bytes 17301512 | tf_op jit(solution)/shard_map/ppermute | solution.py:595
  1264.6 316.6 %reduce-scatter.11.cloned.1.call-start = ((), (), s32[]{:S(2)}) async-start(), calls=%async_computation.11 | async-start | bytes 7864320 | tf_op jit(solution)/shard_map/reduce_scatter | solution.py:734
  1264.6 124.0 %collective-permute-start.59 = (bf16[4,704,1024]{2,1,0:T(8,128)(2,1)}, bf16[4,704,1024]{2,1,0:T(8,128)(2,1)}, u32[]{:S(2)}, u32[]{:S(2)}) collective-permute-start(bf16[4,704,1024]{2,1,0:T(8,128)(2,1)} %add_convert_fusion.3), channel_id=1, source_target_pairs={{0,16},{8,24},{16,0},{24,8},{1,17},{9,25},{17,1},{25,9},{2,18},{10... | collective-permute-start | bytes 17301512 | tf_op jit(solution)/shard_map/ppermute | solution.py:600
  1345.4 89.0 %collective-permute-start.79 = (bf16[704,1024]{1,0:T(8,128)(2,1)}, bf16[704,1024]{1,0:T(8,128)(2,1)}, u32[]{:S(2)}, u32[]{:S(2)}) collective-permute-start(bf16[704,1024]{1,0:T(8,128)(2,1)} %add_convert_fusion.13), channel_id=1, source_target_pairs={{0,8},{8,0},{16,24},{24,16},{1,9},{9,1},{17,25},{25,17},{2,10},{10... | collective-permute-start | bytes 4325384 | tf_op jit(solution)/shard_map/ppermute | solution.py:600
  1449.6 91.5 %collective-permute-start.73 = (bf16[4,704,1024]{2,1,0:T(8,128)(2,1)}, bf16[4,704,1024]{2,1,0:T(8,128)(2,1)}, u32[]{:S(2)}, u32[]{:S(2)}) collective-permute-start(bf16[4,704,1024]{2,1,0:T(8,128)(2,1)} %add_convert_fusion.1), channel_id=1, source_target_pairs={{0,8},{8,0},{16,24},{24,16},{1,9},{9,1},{17,25},{25,17},{2,10},{10... | collective-permute-start | bytes 17301512 | tf_op jit(solution)/shard_map/ppermute | solution.py:600
  1593.2 99.1 %collective-permute-start.68 = (bf16[384,1024]{1,0:T(8,128)(2,1)}, bf16[384,1024]{1,0:T(8,128)(2,1)}, u32[]{:S(2)}, u32[]{:S(2)}) collective-permute-start(bf16[384,1024]{1,0:T(8,128)(2,1)} %slice.275), channel_id=1, source_target_pairs={{0,1},{1,0},{2,3},{3,2},{4,5},{5,4},{6,7},{7,6},{8,9},{9,8},{10,11... | collective-permute-start | bytes 2359304 | tf_op jit(solution)/shard_map/ppermute | solution.py:595
  1594.7 101.8 %collective-permute-start.69 = (bf16[512,1536]{1,0:T(8,128)(2,1)}, bf16[512,1536]{1,0:T(8,128)(2,1)}, u32[]{:S(2)}, u32[]{:S(2)}) collective-permute-start(bf16[512,1536]{1,0:T(8,128)(2,1)} %add_convert_fusion.10), channel_id=1, source_target_pairs={{0,16},{8,24},{16,0},{24,8},{1,17},{9,25},{17,1},{25,9},{2,18},{10... | collective-permute-start | bytes 4718600 | tf_op jit(solution)/shard_map/ppermute | solution.py:600
  1618.4 84.5 %collective-permute-start.71 = (bf16[256,1024]{1,0:T(8,128)(2,1)S(1)}, bf16[256,1024]{1,0:T(8,128)(2,1)}, u32[]{:S(2)}, u32[]{:S(2)}) collective-permute-start(bf16[256,1024]{1,0:T(8,128)(2,1)S(1)} %copy-done.42), channel_id=1, source_target_pairs={{0,16},{8,24},{16,0},{24,8},{1,17},{9,25},{17,1},{25,9},{2,18},{10... | collective-permute-start | bytes 1572872 | tf_op jit(solution)/shard_map/ppermute | solution.py:600
  1621.5 83.5 %collective-permute-start.60 = (bf16[384,1024]{1,0:T(8,128)(2,1)}, bf16[384,1024]{1,0:T(8,128)(2,1)}, u32[]{:S(2)}, u32[]{:S(2)}) collective-permute-start(bf16[384,1024]{1,0:T(8,128)(2,1)} %slice.200), channel_id=1, source_target_pairs={{0,1},{1,0},{2,3},{3,2},{4,5},{5,4},{6,7},{7,6},{8,9},{9,8},{10,11... | collective-permute-start | bytes 2359304 | tf_op jit(solution)/shard_map/ppermute | solution.py:595
  (154 other events, 4935.3 us)
Sparse Core Ops, SparseCore 0:
  58.8 117.1 all-gather.4
  178.2 113.5 all-gather.6
  343.2 108.8 reduce-scatter.4
  456.9 115.8 all-gather.8
  980.5 113.0 reduce-scatter.6
  1117.1 119.5 all-gather.10
  1264.7 110.5 reduce-scatter.8
  1427.6 109.6 reduce-scatter.10
